TPU v7x, 32 devices: a whole 2x2x4 slice. The times are simulated.
32 devices in a mesh: scen: 8 (over z, core), row: 4 (over y, x).
Axes of the slice: x: 2, y: 2, z: 4, core: 2. Of those that a mesh axis runs over, the one named last changes fastest.
Arguments:
- coupling: bfloat16 [8, 1536, 4096], P('scen', None, 'row'), may hold values from -40 to 40
- solves: bfloat16 [8, 1536, 512], P('scen', 'row'), may hold values from -1.25 to 1.25
- border_diagonal: float32 [1024, 4], P('scen', 'row'), may hold values from 32 to 64
- panel_rows: int32 [512], replicated, may hold values from 0 to 4095, as said below
Outputs:
- first_factor: float32 [1024, 4, 256], P('scen', 'row')
- second_factor: float32 [1024, 4, 256], P('scen', 'row')
Inputs may be any that keep to these rules, and one draw needn't show every extreme that they name: `panel_rows`: 512 distinct border rows; the first 256 are the first panel's pivot rows and columns, the rest the second's.
All inputs are finite; a program needn't handle non-finite values. Where the computation divides by a largest or mean magnitude, that divisor is 1e-20 or more.
Results may differ from a plain program's by a relative error of at most 0.0003.
Values may be sent and summed in bfloat16 or wider, within the bound.
No kernel may reach another device: no remote copies, remote signals or barrier semaphores. Data moves between devices by JAX's collectives and lax.ppermute only.
A program may use at most 64 MiB of HBM per device.

v0:
```python
import functools

import jax
import jax.numpy as jnp
from jax import lax
from jax.experimental import pallas as pl
from jax.experimental.pallas import tpu as pltpu
from jax.sharding import PartitionSpec as P

HALF = 256
NEWTON = 8
F32 = jnp.float32
BF16 = jnp.bfloat16


def halves(a):
    high = a.astype(BF16)
    low = (a - high.astype(F32)).astype(BF16)
    return high, low


def left_of(a):
    high, low = halves(a)
    return jnp.concatenate([high, high, low], axis=1)


def right_of(b):
    high, low = halves(b)
    return jnp.concatenate([high, low, high], axis=0)


def dot(a, b):
    return jnp.dot(a, b, preferred_element_type=F32)


def product(a, b):
    return dot(left_of(a), right_of(b))


def newton(pivot):
    size = jnp.abs(pivot)
    norm_one = jnp.max(jnp.sum(size, axis=0, keepdims=True))
    norm_inf = jnp.max(jnp.sum(size, axis=1, keepdims=True))
    approx = pivot.T / (norm_one * norm_inf)
    pivot_right = right_of(pivot)
    for step in range(NEWTON):
        left = dot(left_of(approx), pivot_right)
        approx = 2.0 * approx - product(left, approx)
    return approx


def place_blocks(place_ref, own_ref, other_ref, rows_ref, blocks):
    size = rows_ref.shape[0] // blocks
    for k in range(blocks):
        source = own_ref if k < blocks // 2 else other_ref
        start = k % (blocks // 2) * size
        target = pl.multiple_of((place_ref[0] ^ k) * size, size)
        rows_ref[pl.ds(target, size), :] = source[start:start + size, :]


def first_kernel(blocks, place_ref, own_ref, other_ref, inverse_ref, lower_ref, rows_ref):
    place_blocks(place_ref, own_ref, other_ref, rows_ref, blocks)
    half = inverse_ref.shape[0]
    lower_ref[...] = rows_ref[half:, :]
    inverse_ref[...] = newton(rows_ref[:half, :])


def second_kernel(
    blocks, place_ref, own_ref, other_ref, inverse_first_ref, lower_ref, inverse_ref, upper_ref, rows_ref
):
    place_blocks(place_ref, own_ref, other_ref, rows_ref, blocks)
    half = inverse_ref.shape[0]
    upper = rows_ref[:half, :]
    upper_ref[...] = upper
    lower_factor = product(lower_ref[...], inverse_first_ref[...])
    inverse_ref[...] = newton(rows_ref[half:, :] - product(lower_factor, upper))


def factor_kernel(rows_ref, inverse_first_ref, inverse_second_ref, upper_ref, first_out, second_out):
    half = upper_ref.shape[0]
    first_factor = product(rows_ref[:half, :].T, inverse_first_ref[...])
    updated = rows_ref[half:, :].T - product(first_factor, upper_ref[...])
    first_out[...] = first_factor[:, None, :]
    second_out[...] = product(updated, inverse_second_ref[...])[:, None, :]


def contract(a, b, dims):
    return lax.dot_general(a, b, (dims, ((), ())), preferred_element_type=F32)


def pick_kernel(blocks, place_ref, wanted_ref, own_diagonal_ref, coupling_ref, picked_ref, left_ref, right_ref):
    first_column, first_row, me = place_ref[0], place_ref[1], place_ref[2]
    panel = picked_ref.shape[0]
    columns, share = coupling_ref.shape[1], own_diagonal_ref.shape[1]
    wanted = jnp.broadcast_to(wanted_ref[...], (8, panel)).astype(F32).T[:, :1].astype(jnp.int32)
    here = wanted - first_column == lax.broadcasted_iota(jnp.int32, (panel, columns), 1)
    chosen = jnp.where(here, F32(1.0), F32(0.0)).astype(BF16)
    picked_ref[...] = contract(chosen, coupling_ref[...], ((1,), (1,))).astype(BF16)
    owned = wanted - first_row == lax.broadcasted_iota(jnp.int32, (panel, share), 1)
    entry = jnp.sum(jnp.where(owned, own_diagonal_ref[...], F32(0.0)), axis=1, keepdims=True)
    size = panel // blocks
    half = left_ref.shape[1]
    for k in range(blocks):
        rows = slice(k * size, (k + 1) * size)
        index = lax.broadcasted_iota(jnp.int32, (size, half), 0) + (me ^ k) * size
        column = lax.broadcasted_iota(jnp.int32, (size, half), 1)
        left_ref[rows, :] = jnp.where(index == column, entry[rows], F32(0.0))
        right_ref[rows, :] = jnp.where(index == column + half, entry[rows], F32(0.0))


def pivot_kernel(place_ref, picked_ref, diagonal_ref, *refs):
    *pieces, solves_ref, keep_ref, send_ref = refs
    if len(pieces) == 1:
        solves_ref[...] = pieces[0][...]
    else:
        block, far = pieces[0].shape[0], pieces[3].shape[0]
        for k, offset, piece in zip((0, 1, 2, 3, 3), (0, 0, 0, 0, far), pieces):
            start = pl.multiple_of((place_ref[0] ^ k) * block + offset, far)
            solves_ref[pl.ds(start, piece.shape[0]), :] = piece[...]
    total = dot(picked_ref[...], solves_ref[...]) + diagonal_ref[...]
    half = keep_ref.shape[0]
    keep_ref[...] = total[:half]
    send_ref[...] = total[half:]


def schur_kernel(order, place_ref, coupling_ref, first_ref, second_ref, keep_ref, send_ref, turned_ref):
    layer, core = place_ref[0], place_ref[1]
    half = first_ref.shape[1]
    panel = 2 * half
    turned_ref[:half, :] = first_ref[...].T
    turned_ref[half:, :] = second_ref[...].T
    share = keep_ref.shape[1]
    for position, k in enumerate(order):
        start = pl.multiple_of((layer ^ k) * 2 * share, 2 * share)
        both = dot(turned_ref[...], coupling_ref[:, pl.ds(start, 2 * share)])
        rows = slice(position * panel, (position + 1) * panel)
        one, two = both[:, :share], both[:, share:]
        keep_ref[rows, :] = jnp.where(core == 0, one, two)
        send_ref[rows, :] = jnp.where(core == 0, two, one)


def in_vmem(kernel, out_shape, flops, *args, scratch=(), scalars=0):
    vmem = pl.BlockSpec(memory_space=pltpu.VMEM)
    smem = pl.BlockSpec(memory_space=pltpu.SMEM)
    return pl.pallas_call(
        kernel,
        out_shape=out_shape,
        in_specs=[smem] * scalars + [vmem] * (len(args) - scalars),
        out_specs=jax.tree.map(lambda _: vmem, out_shape),
        scratch_shapes=scratch,
        compiler_params=pltpu.CompilerParams(vmem_limit_bytes=28 * 1024 * 1024),
        cost_estimate=pl.CostEstimate(flops=flops, bytes_accessed=1 << 20, transcendentals=0),
    )(*args)


def swap(x, axis, bit):
    count = lax.axis_size(axis)
    return lax.ppermute(x, axis, [(i, i ^ bit) for i in range(count)])


def after(x, *others):
    return lax.optimization_barrier((x,) + others)[0]


def bits_of(count):
    return [1 << i for i in range(count.bit_length() - 1)]


def gather_pieces(block, rows):
    if rows != 4:
        return [lax.all_gather(block, "row", axis=0, tiled=True)], block
    along_x, along_y = swap(block, "row", 1), swap(block, "row", 2)
    half = block.shape[0] // 2
    far = [swap(along_y[:half], "row", 1), swap(along_x[half:], "row", 2)]
    return [block, along_x, along_y] + far, along_y


def sum_pivots(keep, send, rows, layers):
    part = keep + swap(send, "scen", 1)
    for bit in bits_of(rows):
        half = part.shape[0] // 2
        part = part[:half] + swap(part[half:], "row", bit)
    for bit in bits_of(layers):
        part = part + swap(part, "scen", 2 * bit)
    summed = part
    for bit in reversed(bits_of(rows)):
        part = jnp.concatenate([part, swap(part, "row", bit)], axis=0)
    return part, swap(part, "scen", 1), summed


def shards(coupling, solves, border_diagonal, panel_rows):
    half = HALF
    coupling, solves = coupling[0], solves[0]
    local, row_count = coupling.shape
    block, panel = solves.shape
    scen, rows = lax.axis_size("scen"), lax.axis_size("row")
    layers = scen // 2
    row, place = lax.axis_index("row"), lax.axis_index("scen")
    layer, core = place // 2, place % 2
    share = row_count // scen
    base = row * row_count + place * share

    own_first, own_second = solves[:, :half], solves[:, half:]
    pieces_first, arrived = gather_pieces(own_first, rows)
    pieces_second, _ = gather_pieces(after(own_second, arrived), rows)

    blocks = 2 * rows
    size = panel // blocks
    turned = sum(((row >> i) & 1) << (len(bits_of(rows)) - 1 - i) for i in range(len(bits_of(rows))))
    me = core * rows + turned
    wanted = jnp.concatenate(
        [lax.dynamic_slice_in_dim(panel_rows, (me ^ k) * size, size, 0) for k in range(blocks)]
    )
    places = jnp.stack([row * row_count, base, me]).astype(jnp.int32)
    corner_shape = jax.ShapeDtypeStruct((panel, half), F32)
    picked, *diagonals = in_vmem(
        functools.partial(pick_kernel, blocks),
        (jax.ShapeDtypeStruct((panel, local), BF16), corner_shape, corner_shape),
        2 * panel * row_count * local,
        places, wanted[None, :], border_diagonal.T, coupling, scalars=1,
    )
    glob = base + jnp.arange(share, dtype=jnp.int32)
    diag_part = jnp.where(panel_rows[:, None] == glob[None, :], border_diagonal[:, 0][None, :], F32(0.0))

    piece = jax.ShapeDtypeStruct((panel // 2, half), F32)
    gathered = jax.ShapeDtypeStruct((local, half), BF16)
    chains = []
    for pieces, diag in ((pieces_first, diagonals[0]), (pieces_second, diagonals[1])):
        whole, keep, send = in_vmem(
            pivot_kernel, (gathered, piece, piece), 2 * panel * half * local,
            row.astype(jnp.int32)[None], picked, diag, *pieces, scalars=1,
        )
        chains.append((whole, *sum_pivots(keep, send, rows, layers)))
    (solves_first, first_own, first_other, first_summed), (solves_second, second_own, second_other, _) = chains

    if share % 128:
        solves_all = jnp.concatenate([solves_first, solves_second], axis=1)
        terms = contract(solves_all, coupling, ((0,), (0,)))
        part = lax.psum_scatter(terms, "scen", scatter_dimension=1, tiled=True)
    else:
        where = jnp.stack([layer, core]).astype(jnp.int32)
        order = [int(f"{p:0{len(bits_of(layers))}b}"[::-1], 2) for p in range(layers)]
        rowsum = jax.ShapeDtypeStruct((layers * panel, share), F32)
        keep, send = in_vmem(
            functools.partial(schur_kernel, order), (rowsum, rowsum), 2 * row_count * panel * local,
            where, coupling, solves_first, solves_second, scalars=1, scratch=[pltpu.VMEM((panel, local), BF16)],
        )
        part = keep + swap(send, "scen", 1)
        part = after(part, first_summed)
        for bit in bits_of(layers):
            middle = part.shape[0] // 2
            part = part[:middle] + swap(part[middle:], "scen", 2 * bit)
    own_rows = part + diag_part

    square = jax.ShapeDtypeStruct((half, half), F32)
    scratch = [pltpu.VMEM((panel, half), F32)]
    at = me.astype(jnp.int32)[None]
    inverse_first, lower = in_vmem(
        functools.partial(first_kernel, blocks), (square, square), 2 * 16 * 3 * half**3,
        at, first_own, first_other, scratch=scratch, scalars=1,
    )
    inverse_second, upper = in_vmem(
        functools.partial(second_kernel, blocks), (square, square), 2 * 18 * 3 * half**3,
        at, second_own, second_other, inverse_first, lower, scratch=scratch, scalars=1,
    )
    out = jax.ShapeDtypeStruct((share, 1, half), F32)
    return in_vmem(
        factor_kernel, (out, out), 2 * 9 * share * half**2, own_rows, inverse_first, inverse_second, upper
    )


def solution(mesh):
    placed = (P("scen", None, "row"), P("scen", "row", None), P("scen", "row"), P())
    return jax.shard_map(
        shards,
        mesh=mesh,
        in_specs=placed,
        out_specs=(P("scen", "row", None), P("scen", "row", None)),
        check_vma=False,
    )
```

profile of v0, /device:TPU:0, one launch (start us, length us, event | category | flops | bytes accessed | tf_op | source)
XLA Modules:
  0.0 80.6 jit_solution(18004991761423804502)
XLA Ops:
  0.6 1.0 %fusion.1 = (bf16[384,256]{1,0:T(8,128)(2,1)S(1)}, bf16[384,256]{1,0:T(8,128)(2,1)S(1)}) fusion(bf16[384,512]{1,0:T(8,128)(2,1)} %bitcast.16), kind=kLoop, calls=%fused_computation.14 | loop fusion | bytes 786432 | tf_op jit(solution)/shard_map/slice | solution.py:203
  1.7 3.0 %collective-permute-start.1 = (bf16[384,256]{1,0:T(8,128)(2,1)S(1)}, bf16[384,256]{1,0:T(8,128)(2,1)S(1)}, u32[]{:S(2)}, u32[]{:S(2)}) collective-permute-start(bf16[384,256]{1,0:T(8,128)(2,1)S(1)} %get-tuple-element.37.refs_0_), channel_id=1, source_target_pairs={{0,2},{1,3},{2,0},{3,1},{4,6},{5,7},{6,4},{7,5},{8,10},{9,11},{10,... | collective-permute-start | bytes 589832 | tf_op jit(solution)/shard_map/ppermute | solution.py:158
  4.7 1.5 %collective-permute-start = (bf16[384,256]{1,0:T(8,128)(2,1)S(1)}, bf16[384,256]{1,0:T(8,128)(2,1)S(1)}, u32[]{:S(2)}, u32[]{:S(2)}) collective-permute-start(bf16[384,256]{1,0:T(8,128)(2,1)S(1)} %get-tuple-element.37.refs_0_), channel_id=1, source_target_pairs={{0,1},{1,0},{2,3},{3,2},{4,5},{5,4},{6,7},{7,6},{8,9},{9,8},{10,11... | collective-permute-start | bytes 589832 | tf_op jit(solution)/shard_map/ppermute | solution.py:158
  6.2 1.1 %fusion.2 = (s32[64]{0:T(128)S(1)}, s32[64]{0:T(128)S(1)}, s32[64]{0:T(128)S(1)}, s32[64]{0:T(128)S(1)}, s32[64]{0:T(128)S(1)}, /*index=5*/s32[64]{0:T(128)S(1)}, s32[64]{0:T(128)S(1)}, s32[64]{0:T(128)S(1)}) fusion(s32[512]{0:T(512)} %param.7, s32[]{:T(128)S(6)} %select_n.48, s32[]{:T(128)S(6)} %select_n.47, s32[]{:T(128)S(6)} %select_n.46, ...), kind=kLoop, calls=%fused_computation.15 | loop fusion | bytes 4128 | tf_op jit(solution)/shard_map/dynamic_slice | solution.py:212
  7.3 0.1 concatenate.17
  7.3 0.1 pad_add_fusion.1.place_ref
  7.4 2.2 %collective-permute-done.1.refs_2_ = bf16[384,256]{1,0:T(8,128)(2,1)S(1)} collective-permute-done((bf16[384,256]{1,0:T(8,128)(2,1)S(1)}, bf16[384,256]{1,0:T(8,128)(2,1)S(1)}, u32[]{:S(2)}, u32[]{:S(2)}) %collective-permute-start.1) | collective-permute-done | bytes 196640 | tf_op jit(solution)/shard_map/ppermute | solution.py:158
  9.6 1.7 %collective-permute-start.5 = (bf16[384,256]{1,0:T(8,128)(2,1)S(1)}, bf16[384,256]{1,0:T(8,128)(2,1)S(1)}, u32[]{:S(2)}, u32[]{:S(2)}) collective-permute-start(bf16[384,256]{1,0:T(8,128)(2,1)S(1)} %get-tuple-element.23.refs_0_), channel_id=1, source_target_pairs={{0,2},{1,3},{2,0},{3,1},{4,6},{5,7},{6,4},{7,5},{8,10},{9,11},{10,... | collective-permute-start | bytes 589832 | tf_op jit(solution)/shard_map/ppermute | solution.py:158
  11.4 1.5 %collective-permute-start.4 = (bf16[384,256]{1,0:T(8,128)(2,1)S(1)}, bf16[384,256]{1,0:T(8,128)(2,1)S(1)}, u32[]{:S(2)}, u32[]{:S(2)}) collective-permute-start(bf16[384,256]{1,0:T(8,128)(2,1)S(1)} %get-tuple-element.23.refs_0_), channel_id=1, source_target_pairs={{0,1},{1,0},{2,3},{3,2},{4,5},{5,4},{6,7},{7,6},{8,9},{9,8},{10,11... | collective-permute-start | bytes 589832 | tf_op jit(solution)/shard_map/ppermute | solution.py:158
  12.9 0.6 collective-permute-start.2
  13.5 0.4 collective-permute-start.3
  13.8 0.7 copy-done
  14.5 1.9 %copy-done.2 = bf16[1,1536,1024]{2,1,0:T(8,128)(2,1)S(1)} copy-done((bf16[1,1536,1024]{2,1,0:T(8,128)(2,1)S(1)}, bf16[1,1536,1024]{2,1,0:T(8,128)(2,1)}, u32[]{:S(2)}) %copy-start.2) | copy-done | bytes 3145752
  16.4 2.7 %shard_map.59 = (bf16[512,1536]{1,0:T(8,128)(2,1)S(1)}, f32[512,256]{1,0:T(8,128)S(1)}, f32[512,256]{1,0:T(8,128)S(1)}) custom-call(s32[3]{0:T(128)S(1)} %pad_add_fusion.1.place_ref, s32[1,512]{1,0:T(1,128)S(1)} %bitcast.11, f32[1,128]{1,0:T(1,128)S(1)} %bitcast.12, bf16[1536,1024]{1,0:T(8,128)(2,1)S(1)} %bitcast.14), custom_call_target="tpu_custom_call" | custom-call | flops 1610612736 | bytes 1048576 | tf_op jit(solution)/shard_map/pallas_call | solution.py:145
  19.1 0.0 collective-permute-done.2.refs_3_
  19.1 0.0 collective-permute-done.3.refs_4_
  19.1 1.3 %shard_map.60 = (bf16[1536,256]{1,0:T(8,128)(2,1)S(1)}, f32[256,256]{1,0:T(8,128)S(1)}, f32[256,256]{1,0:T(8,128)}) custom-call(s32[1]{0:T(128)} %bitcast.3.place_ref, bf16[512,1536]{1,0:T(8,128)(2,1)S(1)} %get-tuple-element.19.picked_ref, f32[512,256]{1,0:T(8,128)S(1)} %get-tuple-element.20.diagonal_ref, bf16[384,256]{1,0:T(8,128)(2,1)S(1)} %get-tuple-element.37.refs_0_, ...), custom_call_target="tpu_custom_call" | custom-call | flops 402653184 | bytes 1048576 | tf_op jit(solution)/shard_map/pallas_call | solution.py:145
  20.4 0.9 %copy-done.4 = bf16[1536,256]{1,0:T(8,128)(2,1)} copy-done((bf16[1536,256]{1,0:T(8,128)(2,1)}, bf16[1536,256]{1,0:T(8,128)(2,1)S(1)}, u32[]{:S(2)}) %copy-start.4) | copy-done | bytes 786456
  21.3 0.0 collective-permute-done.5.refs_2_
  21.3 1.8 %collective-permute-start.6 = (bf16[192,256]{1,0:T(8,128)(2,1)S(1)}, bf16[192,256]{1,0:T(8,128)(2,1)S(1)}, u32[]{:S(2)}, u32[]{:S(2)}) collective-permute-start(bf16[192,256]{1,0:T(8,128)(2,1)S(1)} %slice.76), channel_id=1, source_target_pairs={{0,1},{1,0},{2,3},{3,2},{4,5},{5,4},{6,7},{7,6},{8,9},{9,8},{10,11... | collective-permute-start | bytes 294920 | tf_op jit(solution)/shard_map/ppermute | solution.py:158
  23.1 0.0 collective-permute-done.4.refs_1_
  23.1 1.6 %collective-permute-start.7 = (bf16[192,256]{1,0:T(8,128)(2,1)S(1)}, bf16[192,256]{1,0:T(8,128)(2,1)S(1)}, u32[]{:S(2)}, u32[]{:S(2)}) collective-permute-start(bf16[192,256]{1,0:T(8,128)(2,1)S(1)} %slice.77), channel_id=1, source_target_pairs={{0,2},{1,3},{2,0},{3,1},{4,6},{5,7},{6,4},{7,5},{8,10},{9,11},{10,... | collective-permute-start | bytes 294920 | tf_op jit(solution)/shard_map/ppermute | solution.py:158
  24.7 1.9 %collective-permute-done.6.refs_3_ = bf16[192,256]{1,0:T(8,128)(2,1)S(1)} collective-permute-done((bf16[192,256]{1,0:T(8,128)(2,1)S(1)}, bf16[192,256]{1,0:T(8,128)(2,1)S(1)}, u32[]{:S(2)}, u32[]{:S(2)}) %collective-permute-start.6) | collective-permute-done | bytes 98336 | tf_op jit(solution)/shard_map/ppermute | solution.py:158
  26.6 1.5 %collective-permute-done.7.refs_4_ = bf16[192,256]{1,0:T(8,128)(2,1)S(1)} collective-permute-done((bf16[192,256]{1,0:T(8,128)(2,1)S(1)}, bf16[192,256]{1,0:T(8,128)(2,1)S(1)}, u32[]{:S(2)}, u32[]{:S(2)}) %collective-permute-start.7) | collective-permute-done | bytes 98336 | tf_op jit(solution)/shard_map/ppermute | solution.py:158
  28.1 0.6 shard_map.61
  28.8 0.1 collective-permute-start.19
  28.8 0.1 pad_add_fusion.place_ref
  28.9 1.0 %add.103 = f32[256,256]{1,0:T(8,128)S(1)} add(f32[256,256]{1,0:T(8,128)S(1)} %get-tuple-element.27, f32[256,256]{1,0:T(8,128)} %collective-permute-done.9) | non-fusion elementwise | flops 65536 | bytes 786432 | tf_op jit(solution)/shard_map/add | solution.py:179
  29.9 0.4 collective-permute-start.10
  30.3 2.4 %shard_map.62 = (f32[2048,128]{1,0:T(8,128)S(1)}, f32[2048,128]{1,0:T(8,128)S(1)}) custom-call(s32[2]{0:T(128)S(1)} %pad_add_fusion.place_ref, bf16[1536,1024]{1,0:T(8,128)(2,1)S(1)} %bitcast.15, bf16[1536,256]{1,0:T(8,128)(2,1)S(1)} %copy-done.5, bf16[1536,256]{1,0:T(8,128)(2,1)S(1)} %get-tuple-element.24.second_ref), custom_call_target="tpu_custom_call" | custom-call | flops 1610612736 | bytes 1048576 | tf_op jit(solution)/shard_map/pallas_call | solution.py:145
  32.7 0.3 collective-permute-start.8
  33.0 1.8 %collective-permute-start.20 = (f32[128,256]{1,0:T(8,128)S(1)}, f32[128,256]{1,0:T(8,128)S(1)}, u32[]{:S(2)}, u32[]{:S(2)}) collective-permute-start(f32[128,256]{1,0:T(8,128)S(1)} %slice.85), channel_id=1, source_target_pairs={{0,1},{1,0},{2,3},{3,2},{4,5},{5,4},{6,7},{7,6},{8,9},{9,8},{10,11... | collective-permute-start | bytes 393224 | tf_op jit(solution)/shard_map/ppermute | solution.py:158
  34.8 1.1 %collective-permute-done.10 = f32[128,256]{1,0:T(8,128)S(1)} collective-permute-done((f32[128,256]{1,0:T(8,128)S(1)}, f32[128,256]{1,0:T(8,128)S(1)}, u32[]{:S(2)}, u32[]{:S(2)}) %collective-permute-start.10) | collective-permute-done | bytes 131104 | tf_op jit(solution)/shard_map/ppermute | solution.py:158
  35.9 1.6 %collective-permute-start.11 = (f32[64,256]{1,0:T(8,128)S(1)}, f32[64,256]{1,0:T(8,128)S(1)}, u32[]{:S(2)}, u32[]{:S(2)}) collective-permute-start(f32[64,256]{1,0:T(8,128)S(1)} %slice.81), channel_id=1, source_target_pairs={{0,2},{1,3},{2,0},{3,1},{4,6},{5,7},{6,4},{7,5},{8,10},{9,11},{10,... | collective-permute-start | bytes 196616 | tf_op jit(solution)/shard_map/ppermute | solution.py:158
  37.5 1.3 %collective-permute-done.20 = f32[128,256]{1,0:T(8,128)S(1)} collective-permute-done((f32[128,256]{1,0:T(8,128)S(1)}, f32[128,256]{1,0:T(8,128)S(1)}, u32[]{:S(2)}, u32[]{:S(2)}) %collective-permute-start.20) | collective-permute-done | bytes 131104 | tf_op jit(solution)/shard_map/ppermute | solution.py:158
  38.8 1.8 %collective-permute-start.21 = (f32[64,256]{1,0:T(8,128)S(1)}, f32[64,256]{1,0:T(8,128)S(1)}, u32[]{:S(2)}, u32[]{:S(2)}) collective-permute-start(f32[64,256]{1,0:T(8,128)S(1)} %slice.87), channel_id=1, source_target_pairs={{0,2},{1,3},{2,0},{3,1},{4,6},{5,7},{6,4},{7,5},{8,10},{9,11},{10,... | collective-permute-start | bytes 196616 | tf_op jit(solution)/shard_map/ppermute | solution.py:158
  40.6 1.6 %collective-permute-start.12 = (f32[64,256]{1,0:T(8,128)S(1)}, f32[64,256]{1,0:T(8,128)S(1)}, u32[]{:S(2)}, u32[]{:S(2)}) collective-permute-start(f32[64,256]{1,0:T(8,128)S(1)} %slice_add_fusion.5), channel_id=1, source_target_pairs={{0,8},{4,12},{8,0},{12,4},{16,24},{20,28},{24,16},{28,20},{1,9},{5... | collective-permute-start | bytes 196616 | tf_op jit(solution)/shard_map/ppermute | solution.py:158
  42.3 0.9 %collective-permute-done.21 = f32[64,256]{1,0:T(8,128)S(1)} collective-permute-done((f32[64,256]{1,0:T(8,128)S(1)}, f32[64,256]{1,0:T(8,128)S(1)}, u32[]{:S(2)}, u32[]{:S(2)}) %collective-permute-start.21) | collective-permute-done | bytes 65568 | tf_op jit(solution)/shard_map/ppermute | solution.py:158
  43.2 1.9 %collective-permute-start.22 = (f32[64,256]{1,0:T(8,128)S(1)}, f32[64,256]{1,0:T(8,128)S(1)}, u32[]{:S(2)}, u32[]{:S(2)}) collective-permute-start(f32[64,256]{1,0:T(8,128)S(1)} %slice_add_fusion.4), channel_id=1, source_target_pairs={{0,8},{4,12},{8,0},{12,4},{16,24},{20,28},{24,16},{28,20},{1,9},{5... | collective-permute-start | bytes 196616 | tf_op jit(solution)/shard_map/ppermute | solution.py:158
  45.1 0.6 collective-permute-done.12
  45.7 2.6 %collective-permute-start.13 = (f32[64,256]{1,0:T(8,128)S(1)}, f32[64,256]{1,0:T(8,128)S(1)}, u32[]{:S(2)}, u32[]{:S(2)}) collective-permute-start(f32[64,256]{1,0:T(8,128)S(1)} %add.106), channel_id=1, source_target_pairs={{0,16},{4,20},{8,24},{12,28},{16,0},{20,4},{24,8},{28,12},{1,17},{... | collective-permute-start | bytes 196616 | tf_op jit(solution)/shard_map/ppermute | solution.py:158
  48.3 2.1 %collective-permute-start.23 = (f32[64,256]{1,0:T(8,128)S(1)}, f32[64,256]{1,0:T(8,128)S(1)}, u32[]{:S(2)}, u32[]{:S(2)}) collective-permute-start(f32[64,256]{1,0:T(8,128)S(1)} %add.116), channel_id=1, source_target_pairs={{0,16},{4,20},{8,24},{12,28},{16,0},{20,4},{24,8},{28,12},{1,17},{... | collective-permute-start | bytes 196616 | tf_op jit(solution)/shard_map/ppermute | solution.py:158
  50.4 1.9 %collective-permute-done.13 = f32[64,256]{1,0:T(8,128)S(1)} collective-permute-done((f32[64,256]{1,0:T(8,128)S(1)}, f32[64,256]{1,0:T(8,128)S(1)}, u32[]{:S(2)}, u32[]{:S(2)}) %collective-permute-start.13) | collective-permute-done | bytes 65568 | tf_op jit(solution)/shard_map/ppermute | solution.py:158
  52.3 1.2 %collective-permute-start.16 = (f32[64,256]{1,0:T(8,128)S(1)}, f32[64,256]{1,0:T(8,128)S(1)}, u32[]{:S(2)}, u32[]{:S(2)}) collective-permute-start(f32[64,256]{1,0:T(8,128)S(1)} %add.107), channel_id=1, source_target_pairs={{0,2},{1,3},{2,0},{3,1},{4,6},{5,7},{6,4},{7,5},{8,10},{9,11},{10,... | collective-permute-start | bytes 196616 | tf_op jit(solution)/shard_map/ppermute | solution.py:158
  53.5 0.0 collective-permute-done.23
  53.5 1.4 %collective-permute-start.24 = (f32[64,256]{1,0:T(8,128)S(1)}, f32[64,256]{1,0:T(8,128)S(1)}, u32[]{:S(2)}, u32[]{:S(2)}) collective-permute-start(f32[64,256]{1,0:T(8,128)S(1)} %add.117), channel_id=1, source_target_pairs={{0,2},{1,3},{2,0},{3,1},{4,6},{5,7},{6,4},{7,5},{8,10},{9,11},{10,... | collective-permute-start | bytes 196616 | tf_op jit(solution)/shard_map/ppermute | solution.py:158
  54.9 0.1 add.102
  55.1 1.8 %collective-permute-start.14 = (f32[1024,128]{1,0:T(8,128)S(1)}, f32[1024,128]{1,0:T(8,128)S(1)}, u32[]{:S(2)}, u32[]{:S(2)}) collective-permute-start(f32[1024,128]{1,0:T(8,128)S(1)} %slice.65), channel_id=1, source_target_pairs={{0,8},{4,12},{8,0},{12,4},{16,24},{20,28},{24,16},{28,20},{1,9},{5... | collective-permute-start | bytes 1572872 | tf_op jit(solution)/shard_map/ppermute | solution.py:158
  56.9 1.6 %collective-permute-start.17 = (f32[128,256]{1,0:T(8,128)S(1)}, f32[128,256]{1,0:T(8,128)S(1)}, u32[]{:S(2)}, u32[]{:S(2)}) collective-permute-start(f32[128,256]{1,0:T(8,128)S(1)} %pad_maximum_fusion.2), channel_id=1, source_target_pairs={{0,1},{1,0},{2,3},{3,2},{4,5},{5,4},{6,7},{7,6},{8,9},{9,8},{10,11... | collective-permute-start | bytes 393224 | tf_op jit(solution)/shard_map/ppermute | solution.py:158
  58.4 1.0 %collective-permute-start.25 = (f32[128,256]{1,0:T(8,128)S(1)}, f32[128,256]{1,0:T(8,128)S(1)}, u32[]{:S(2)}, u32[]{:S(2)}) collective-permute-start(f32[128,256]{1,0:T(8,128)S(1)} %pad_maximum_fusion.3), channel_id=1, source_target_pairs={{0,1},{1,0},{2,3},{3,2},{4,5},{5,4},{6,7},{7,6},{8,9},{9,8},{10,11... | collective-permute-start | bytes 393224 | tf_op jit(solution)/shard_map/ppermute | solution.py:158
  59.5 2.4 %collective-permute-done.17 = f32[128,256]{1,0:T(8,128)S(1)} collective-permute-done((f32[128,256]{1,0:T(8,128)S(1)}, f32[128,256]{1,0:T(8,128)S(1)}, u32[]{:S(2)}, u32[]{:S(2)}) %collective-permute-start.17) | collective-permute-done | bytes 131104 | tf_op jit(solution)/shard_map/ppermute | solution.py:158
  61.9 0.1 collective-permute-start.18
  62.0 1.5 %collective-permute-done.25 = f32[128,256]{1,0:T(8,128)S(1)} collective-permute-done((f32[128,256]{1,0:T(8,128)S(1)}, f32[128,256]{1,0:T(8,128)S(1)}, u32[]{:S(2)}, u32[]{:S(2)}) %collective-permute-start.25) | collective-permute-done | bytes 131104 | tf_op jit(solution)/shard_map/ppermute | solution.py:158
  63.5 0.1 collective-permute-start.26
  63.6 3.4 %collective-permute-done.14 = f32[1024,128]{1,0:T(8,128)S(1)} collective-permute-done((f32[1024,128]{1,0:T(8,128)S(1)}, f32[1024,128]{1,0:T(8,128)S(1)}, u32[]{:S(2)}, u32[]{:S(2)}) %collective-permute-start.14) | collective-permute-done | bytes 524320 | tf_op jit(solution)/shard_map/ppermute | solution.py:158
  67.0 0.1 slice_add_fusion
  67.0 2.5 %collective-permute-start.15 = (f32[512,128]{1,0:T(8,128)S(1)}, f32[512,128]{1,0:T(8,128)S(1)}, u32[]{:S(2)}, u32[]{:S(2)}) collective-permute-start(f32[512,128]{1,0:T(8,128)S(1)} %slice.83), channel_id=1, source_target_pairs={{0,16},{4,20},{8,24},{12,28},{16,0},{20,4},{24,8},{28,12},{1,17},{... | collective-permute-start | bytes 786440 | tf_op jit(solution)/shard_map/ppermute | solution.py:158
  69.6 4.3 %shard_map.63 = (f32[256,256]{1,0:T(8,128)S(1)}, f32[256,256]{1,0:T(8,128)S(1)}) custom-call(s32[1]{0:T(128)} %bitcast.6.place_ref, f32[256,256]{1,0:T(8,128)S(1)} %pad_maximum_fusion.own_ref, f32[256,256]{1,0:T(8,128)S(1)} %collective-permute-done.18.other_ref), custom_call_target="tpu_custom_call" | custom-call | flops 1610612736 | bytes 1048576 | tf_op jit(solution)/shard_map/pallas_call | solution.py:145
  73.9 0.0 copy-start.1
  73.9 0.0 copy-start.6
  73.9 4.9 %shard_map.64 = (f32[256,256]{1,0:T(8,128)S(1)}, f32[256,256]{1,0:T(8,128)S(1)}) custom-call(s32[1]{0:T(128)} %bitcast.6.place_ref, f32[256,256]{1,0:T(8,128)S(1)} %pad_maximum_fusion.1.own_ref, f32[256,256]{1,0:T(8,128)S(1)} %collective-permute-done.26.other_ref, f32[256,256]{1,0:T(8,128)S(1)} %get-tuple-element.30.inverse_first_ref, ...), custom_call_target="tpu_custom_call" | custom-call | flops 1811939328 | bytes 1048576 | tf_op jit(solution)/shard_map/pallas_call | solution.py:145
  78.9 0.3 collective-permute-done.15
  79.1 0.1 fusion.rows_ref
  79.3 1.3 %shard_map.65 = (f32[128,1,256]{2,1,0:T(1,128)}, f32[128,1,256]{2,1,0:T(1,128)}) custom-call(f32[512,128]{1,0:T(8,128)S(1)} %fusion.rows_ref, f32[256,256]{1,0:T(8,128)S(1)} %get-tuple-element.30.inverse_first_ref, f32[256,256]{1,0:T(8,128)S(1)} %get-tuple-element.34.inverse_second_ref, f32[256,256]{1,0:T(8,128)S(1)} %get-tuple-element.35.upper_ref), custom_call_target="tpu_custom_call" | custom-call | flops 150994944 | bytes 1048576 | tf_op jit(solution)/shard_map/pallas_call | solution.py:145
  (44 shorter events, 0.3 us)
Async XLA Ops:
  1.7 7.9 %collective-permute-start.1 = (bf16[384,256]{1,0:T(8,128)(2,1)S(1)}, bf16[384,256]{1,0:T(8,128)(2,1)S(1)}, u32[]{:S(2)}, u32[]{:S(2)}) collective-permute-start(bf16[384,256]{1,0:T(8,128)(2,1)S(1)} %get-tuple-element.37.refs_0_), channel_id=1, source_target_pairs={{0,2},{1,3},{2,0},{3,1},{4,6},{5,7},{6,4},{7,5},{8,10},{9,11},{10,... | collective-permute-start | bytes 589832 | tf_op jit(solution)/shard_map/ppermute | solution.py:158
  4.7 8.7 %collective-permute-start = (bf16[384,256]{1,0:T(8,128)(2,1)S(1)}, bf16[384,256]{1,0:T(8,128)(2,1)S(1)}, u32[]{:S(2)}, u32[]{:S(2)}) collective-permute-start(bf16[384,256]{1,0:T(8,128)(2,1)S(1)} %get-tuple-element.37.refs_0_), channel_id=1, source_target_pairs={{0,1},{1,0},{2,3},{3,2},{4,5},{5,4},{6,7},{7,6},{8,9},{9,8},{10,11... | collective-permute-start | bytes 589832 | tf_op jit(solution)/shard_map/ppermute | solution.py:158
  9.6 11.7 %collective-permute-start.5 = (bf16[384,256]{1,0:T(8,128)(2,1)S(1)}, bf16[384,256]{1,0:T(8,128)(2,1)S(1)}, u32[]{:S(2)}, u32[]{:S(2)}) collective-permute-start(bf16[384,256]{1,0:T(8,128)(2,1)S(1)} %get-tuple-element.23.refs_0_), channel_id=1, source_target_pairs={{0,2},{1,3},{2,0},{3,1},{4,6},{5,7},{6,4},{7,5},{8,10},{9,11},{10,... | collective-permute-start | bytes 589832 | tf_op jit(solution)/shard_map/ppermute | solution.py:158
  11.4 11.8 %collective-permute-start.4 = (bf16[384,256]{1,0:T(8,128)(2,1)S(1)}, bf16[384,256]{1,0:T(8,128)(2,1)S(1)}, u32[]{:S(2)}, u32[]{:S(2)}) collective-permute-start(bf16[384,256]{1,0:T(8,128)(2,1)S(1)} %get-tuple-element.23.refs_0_), channel_id=1, source_target_pairs={{0,1},{1,0},{2,3},{3,2},{4,5},{5,4},{6,7},{7,6},{8,9},{9,8},{10,11... | collective-permute-start | bytes 589832 | tf_op jit(solution)/shard_map/ppermute | solution.py:158
  12.9 6.2 %collective-permute-start.2 = (bf16[192,256]{1,0:T(8,128)(2,1)S(1)}, bf16[192,256]{1,0:T(8,128)(2,1)S(1)}, u32[]{:S(2)}, u32[]{:S(2)}) collective-permute-start(bf16[192,256]{1,0:T(8,128)(2,1)S(1)} %slice.73), channel_id=1, source_target_pairs={{0,1},{1,0},{2,3},{3,2},{4,5},{5,4},{6,7},{7,6},{8,9},{9,8},{10,11... | collective-permute-start | bytes 294920 | tf_op jit(solution)/shard_map/ppermute | solution.py:158
  13.5 5.6 %collective-permute-start.3 = (bf16[192,256]{1,0:T(8,128)(2,1)S(1)}, bf16[192,256]{1,0:T(8,128)(2,1)S(1)}, u32[]{:S(2)}, u32[]{:S(2)}) collective-permute-start(bf16[192,256]{1,0:T(8,128)(2,1)S(1)} %slice.74), channel_id=1, source_target_pairs={{0,2},{1,3},{2,0},{3,1},{4,6},{5,7},{6,4},{7,5},{8,10},{9,11},{10,... | collective-permute-start | bytes 294920 | tf_op jit(solution)/shard_map/ppermute | solution.py:158
  13.8 0.7 copy-start
  14.5 1.9 %copy-start.2 = (bf16[1,1536,1024]{2,1,0:T(8,128)(2,1)S(1)}, bf16[1,1536,1024]{2,1,0:T(8,128)(2,1)}, u32[]{:S(2)}) copy-start(bf16[1,1536,1024]{2,1,0:T(8,128)(2,1)} %param.4) | copy-start | bytes 9437188
  20.4 0.9 %copy-start.4 = (bf16[1536,256]{1,0:T(8,128)(2,1)}, bf16[1536,256]{1,0:T(8,128)(2,1)S(1)}, u32[]{:S(2)}) copy-start(bf16[1536,256]{1,0:T(8,128)(2,1)S(1)} %get-tuple-element.21.first_ref) | copy-start | bytes 2359300
  21.3 7.6 %collective-permute-start.9 = (f32[256,256]{1,0:T(8,128)}, f32[256,256]{1,0:T(8,128)}, u32[]{:S(2)}, u32[]{:S(2)}) collective-permute-start(f32[256,256]{1,0:T(8,128)} %get-tuple-element.28), channel_id=1, source_target_pairs={{0,4},{4,0},{8,12},{12,8},{16,20},{20,16},{24,28},{28,24},{1,5},{5... | collective-permute-start | bytes 786440 | tf_op jit(solution)/shard_map/ppermute | solution.py:158
  21.3 5.3 %collective-permute-start.6 = (bf16[192,256]{1,0:T(8,128)(2,1)S(1)}, bf16[192,256]{1,0:T(8,128)(2,1)S(1)}, u32[]{:S(2)}, u32[]{:S(2)}) collective-permute-start(bf16[192,256]{1,0:T(8,128)(2,1)S(1)} %slice.76), channel_id=1, source_target_pairs={{0,1},{1,0},{2,3},{3,2},{4,5},{5,4},{6,7},{7,6},{8,9},{9,8},{10,11... | collective-permute-start | bytes 294920 | tf_op jit(solution)/shard_map/ppermute | solution.py:158
  23.1 5.0 %collective-permute-start.7 = (bf16[192,256]{1,0:T(8,128)(2,1)S(1)}, bf16[192,256]{1,0:T(8,128)(2,1)S(1)}, u32[]{:S(2)}, u32[]{:S(2)}) collective-permute-start(bf16[192,256]{1,0:T(8,128)(2,1)S(1)} %slice.77), channel_id=1, source_target_pairs={{0,2},{1,3},{2,0},{3,1},{4,6},{5,7},{6,4},{7,5},{8,10},{9,11},{10,... | collective-permute-start | bytes 294920 | tf_op jit(solution)/shard_map/ppermute | solution.py:158
  24.7 5.6 %copy-start.3 = (bf16[1,1536,1024]{2,1,0:T(8,128)(2,1)S(1)}, bf16[1,1536,1024]{2,1,0:T(8,128)(2,1)}, u32[]{:S(2)}) copy-start(bf16[1,1536,1024]{2,1,0:T(8,128)(2,1)} %param.4) | copy-start | bytes 9437188
  24.7 5.6 %copy-start.5 = (bf16[1536,256]{1,0:T(8,128)(2,1)S(1)}, bf16[1536,256]{1,0:T(8,128)(2,1)}, u32[]{:S(2)}) copy-start(bf16[1536,256]{1,0:T(8,128)(2,1)} %copy-done.4) | copy-start | bytes 2359300
  28.8 4.2 %collective-permute-start.19 = (f32[256,256]{1,0:T(8,128)S(1)}, f32[256,256]{1,0:T(8,128)S(1)}, u32[]{:S(2)}, u32[]{:S(2)}) collective-permute-start(f32[256,256]{1,0:T(8,128)S(1)} %get-tuple-element.32), channel_id=1, source_target_pairs={{0,4},{4,0},{8,12},{12,8},{16,20},{20,16},{24,28},{28,24},{1,5},{5... | collective-permute-start | bytes 786440 | tf_op jit(solution)/shard_map/ppermute | solution.py:158
  29.9 6.0 %collective-permute-start.10 = (f32[128,256]{1,0:T(8,128)S(1)}, f32[128,256]{1,0:T(8,128)S(1)}, u32[]{:S(2)}, u32[]{:S(2)}) collective-permute-start(f32[128,256]{1,0:T(8,128)S(1)} %slice.79), channel_id=1, source_target_pairs={{0,1},{1,0},{2,3},{3,2},{4,5},{5,4},{6,7},{7,6},{8,9},{9,8},{10,11... | collective-permute-start | bytes 393224 | tf_op jit(solution)/shard_map/ppermute | solution.py:158
  32.7 22.2 %collective-permute-start.8 = (f32[2048,128]{1,0:T(8,128)S(1)}, f32[2048,128]{1,0:T(8,128)S(1)}, u32[]{:S(2)}, u32[]{:S(2)}) collective-permute-start(f32[2048,128]{1,0:T(8,128)S(1)} %get-tuple-element.26), channel_id=1, source_target_pairs={{0,4},{4,0},{8,12},{12,8},{16,20},{20,16},{24,28},{28,24},{1,5},{5... | collective-permute-start | bytes 3145736 | tf_op jit(solution)/shard_map/ppermute | solution.py:158
  33.0 5.8 %collective-permute-start.20 = (f32[128,256]{1,0:T(8,128)S(1)}, f32[128,256]{1,0:T(8,128)S(1)}, u32[]{:S(2)}, u32[]{:S(2)}) collective-permute-start(f32[128,256]{1,0:T(8,128)S(1)} %slice.85), channel_id=1, source_target_pairs={{0,1},{1,0},{2,3},{3,2},{4,5},{5,4},{6,7},{7,6},{8,9},{9,8},{10,11... | collective-permute-start | bytes 393224 | tf_op jit(solution)/shard_map/ppermute | solution.py:158
  35.9 4.7 %collective-permute-start.11 = (f32[64,256]{1,0:T(8,128)S(1)}, f32[64,256]{1,0:T(8,128)S(1)}, u32[]{:S(2)}, u32[]{:S(2)}) collective-permute-start(f32[64,256]{1,0:T(8,128)S(1)} %slice.81), channel_id=1, source_target_pairs={{0,2},{1,3},{2,0},{3,1},{4,6},{5,7},{6,4},{7,5},{8,10},{9,11},{10,... | collective-permute-start | bytes 196616 | tf_op jit(solution)/shard_map/ppermute | solution.py:158
  38.8 4.3 %collective-permute-start.21 = (f32[64,256]{1,0:T(8,128)S(1)}, f32[64,256]{1,0:T(8,128)S(1)}, u32[]{:S(2)}, u32[]{:S(2)}) collective-permute-start(f32[64,256]{1,0:T(8,128)S(1)} %slice.87), channel_id=1, source_target_pairs={{0,2},{1,3},{2,0},{3,1},{4,6},{5,7},{6,4},{7,5},{8,10},{9,11},{10,... | collective-permute-start | bytes 196616 | tf_op jit(solution)/shard_map/ppermute | solution.py:158
  40.6 5.0 %collective-permute-start.12 = (f32[64,256]{1,0:T(8,128)S(1)}, f32[64,256]{1,0:T(8,128)S(1)}, u32[]{:S(2)}, u32[]{:S(2)}) collective-permute-start(f32[64,256]{1,0:T(8,128)S(1)} %slice_add_fusion.5), channel_id=1, source_target_pairs={{0,8},{4,12},{8,0},{12,4},{16,24},{20,28},{24,16},{28,20},{1,9},{5... | collective-permute-start | bytes 196616 | tf_op jit(solution)/shard_map/ppermute | solution.py:158
  43.2 5.1 %collective-permute-start.22 = (f32[64,256]{1,0:T(8,128)S(1)}, f32[64,256]{1,0:T(8,128)S(1)}, u32[]{:S(2)}, u32[]{:S(2)}) collective-permute-start(f32[64,256]{1,0:T(8,128)S(1)} %slice_add_fusion.4), channel_id=1, source_target_pairs={{0,8},{4,12},{8,0},{12,4},{16,24},{20,28},{24,16},{28,20},{1,9},{5... | collective-permute-start | bytes 196616 | tf_op jit(solution)/shard_map/ppermute | solution.py:158
  45.7 6.6 %collective-permute-start.13 = (f32[64,256]{1,0:T(8,128)S(1)}, f32[64,256]{1,0:T(8,128)S(1)}, u32[]{:S(2)}, u32[]{:S(2)}) collective-permute-start(f32[64,256]{1,0:T(8,128)S(1)} %add.106), channel_id=1, source_target_pairs={{0,16},{4,20},{8,24},{12,28},{16,0},{20,4},{24,8},{28,12},{1,17},{... | collective-permute-start | bytes 196616 | tf_op jit(solution)/shard_map/ppermute | solution.py:158
  48.3 5.2 %collective-permute-start.23 = (f32[64,256]{1,0:T(8,128)S(1)}, f32[64,256]{1,0:T(8,128)S(1)}, u32[]{:S(2)}, u32[]{:S(2)}) collective-permute-start(f32[64,256]{1,0:T(8,128)S(1)} %add.116), channel_id=1, source_target_pairs={{0,16},{4,20},{8,24},{12,28},{16,0},{20,4},{24,8},{28,12},{1,17},{... | collective-permute-start | bytes 196616 | tf_op jit(solution)/shard_map/ppermute | solution.py:158
  52.3 4.5 %collective-permute-start.16 = (f32[64,256]{1,0:T(8,128)S(1)}, f32[64,256]{1,0:T(8,128)S(1)}, u32[]{:S(2)}, u32[]{:S(2)}) collective-permute-start(f32[64,256]{1,0:T(8,128)S(1)} %add.107), channel_id=1, source_target_pairs={{0,2},{1,3},{2,0},{3,1},{4,6},{5,7},{6,4},{7,5},{8,10},{9,11},{10,... | collective-permute-start | bytes 196616 | tf_op jit(solution)/shard_map/ppermute | solution.py:158
  53.5 4.9 %collective-permute-start.24 = (f32[64,256]{1,0:T(8,128)S(1)}, f32[64,256]{1,0:T(8,128)S(1)}, u32[]{:S(2)}, u32[]{:S(2)}) collective-permute-start(f32[64,256]{1,0:T(8,128)S(1)} %add.117), channel_id=1, source_target_pairs={{0,2},{1,3},{2,0},{3,1},{4,6},{5,7},{6,4},{7,5},{8,10},{9,11},{10,... | collective-permute-start | bytes 196616 | tf_op jit(solution)/shard_map/ppermute | solution.py:158
  55.1 11.9 %collective-permute-start.14 = (f32[1024,128]{1,0:T(8,128)S(1)}, f32[1024,128]{1,0:T(8,128)S(1)}, u32[]{:S(2)}, u32[]{:S(2)}) collective-permute-start(f32[1024,128]{1,0:T(8,128)S(1)} %slice.65), channel_id=1, source_target_pairs={{0,8},{4,12},{8,0},{12,4},{16,24},{20,28},{24,16},{28,20},{1,9},{5... | collective-permute-start | bytes 1572872 | tf_op jit(solution)/shard_map/ppermute | solution.py:158
  56.9 5.0 %collective-permute-start.17 = (f32[128,256]{1,0:T(8,128)S(1)}, f32[128,256]{1,0:T(8,128)S(1)}, u32[]{:S(2)}, u32[]{:S(2)}) collective-permute-start(f32[128,256]{1,0:T(8,128)S(1)} %pad_maximum_fusion.2), channel_id=1, source_target_pairs={{0,1},{1,0},{2,3},{3,2},{4,5},{5,4},{6,7},{7,6},{8,9},{9,8},{10,11... | collective-permute-start | bytes 393224 | tf_op jit(solution)/shard_map/ppermute | solution.py:158
  58.4 5.0 %collective-permute-start.25 = (f32[128,256]{1,0:T(8,128)S(1)}, f32[128,256]{1,0:T(8,128)S(1)}, u32[]{:S(2)}, u32[]{:S(2)}) collective-permute-start(f32[128,256]{1,0:T(8,128)S(1)} %pad_maximum_fusion.3), channel_id=1, source_target_pairs={{0,1},{1,0},{2,3},{3,2},{4,5},{5,4},{6,7},{7,6},{8,9},{9,8},{10,11... | collective-permute-start | bytes 393224 | tf_op jit(solution)/shard_map/ppermute | solution.py:158
  61.9 7.6 %collective-permute-start.18 = (f32[256,256]{1,0:T(8,128)S(1)}, f32[256,256]{1,0:T(8,128)S(1)}, u32[]{:S(2)}, u32[]{:S(2)}) collective-permute-start(f32[256,256]{1,0:T(8,128)S(1)} %pad_maximum_fusion.own_ref), channel_id=1, source_target_pairs={{0,4},{4,0},{8,12},{12,8},{16,20},{20,16},{24,28},{28,24},{1,5},{5... | collective-permute-start | bytes 786440 | tf_op jit(solution)/shard_map/ppermute | solution.py:158
  63.5 10.4 %collective-permute-start.26 = (f32[256,256]{1,0:T(8,128)S(1)}, f32[256,256]{1,0:T(8,128)S(1)}, u32[]{:S(2)}, u32[]{:S(2)}) collective-permute-start(f32[256,256]{1,0:T(8,128)S(1)} %pad_maximum_fusion.1.own_ref), channel_id=1, source_target_pairs={{0,4},{4,0},{8,12},{12,8},{16,20},{20,16},{24,28},{28,24},{1,5},{5... | collective-permute-start | bytes 786440 | tf_op jit(solution)/shard_map/ppermute | solution.py:158
  67.0 12.1 %collective-permute-start.15 = (f32[512,128]{1,0:T(8,128)S(1)}, f32[512,128]{1,0:T(8,128)S(1)}, u32[]{:S(2)}, u32[]{:S(2)}) collective-permute-start(f32[512,128]{1,0:T(8,128)S(1)} %slice.83), channel_id=1, source_target_pairs={{0,16},{4,20},{8,24},{12,28},{16,0},{20,4},{24,8},{28,12},{1,17},{... | collective-permute-start | bytes 786440 | tf_op jit(solution)/shard_map/ppermute | solution.py:158
  73.9 5.2 %copy-start.1 = (f32[128,1]{0,1:T(1,128)S(1)}, f32[128,1]{0,1:T(1,128)}, u32[]{:S(2)}) copy-start(f32[128,1]{0,1:T(1,128)} %param.6) | copy-start | bytes 1540
  73.9 5.2 %copy-start.6 = (s32[512]{0:T(512)S(1)}, s32[512]{0:T(512)}, u32[]{:S(2)}) copy-start(s32[512]{0:T(512)} %param.7) | copy-start | bytes 6148
where the time goes:
time: 80.9 us; the launch traced here: 80.6 us
  starting transfers between devices  35.8 us (44%)
  waiting for transfers between devices  18.9 us (23%)
  Pallas kernels  17.6 us (22%)
  local copies, waits for them, and re-layouts  5.76 us (7%)
  other arithmetic  1.62 us (2%)
  between operations  0.89 us (1%)
    ppermute x27, starting transfers between devices, swap(): return lax.ppermute(x, axis, [(i, i ^ bit) for i in range(count)])  35.8 us
    ppermute x27, waiting for transfers between devices, swap(): return lax.ppermute(x, axis, [(i, i ^ bit) for i in range(count)])  18.9 us
    pallas_call x7, Pallas kernels, in_vmem(): pl.pallas_call(kernel, out_shape=out_shape, in_specs=[smem] * scalars + [...  17.6 us
    unnamed x14, local copies, waits for them, and re-layouts  3.45 us
  transfers between devices with their start and end apart: 27, of which 12 were waited for; matrix products, arithmetic and copies ran while one was open for 3% of the time, Pallas kernels for 20%

commit v1 on v0

v1 whole, which is shorter than its diff:
```python
import functools

import jax
import jax.numpy as jnp
from jax import lax
from jax.experimental import pallas as pl
from jax.experimental.pallas import tpu as pltpu
from jax.sharding import PartitionSpec as P

HALF = 256
NEWTON = 8
STEPS = 4
LARGE = 61 << 20
NEWTON_BYTES = 16 << 20
F32 = jnp.float32
BF16 = jnp.bfloat16


def halves(a):
    high = a.astype(BF16)
    low = (a - high.astype(F32)).astype(BF16)
    return high, low


def left_of(a):
    high, low = halves(a)
    return jnp.concatenate([high, high, low], axis=1)


def right_of(b):
    high, low = halves(b)
    return jnp.concatenate([high, low, high], axis=0)


def dot(a, b):
    return jnp.dot(a, b, preferred_element_type=F32)


def product(a, b):
    return dot(left_of(a), right_of(b))


def newton(pivot):
    size = jnp.abs(pivot)
    norm_one = jnp.max(jnp.sum(size, axis=0, keepdims=True))
    norm_inf = jnp.max(jnp.sum(size, axis=1, keepdims=True))
    approx = pivot.T / (norm_one * norm_inf)
    pivot_right = right_of(pivot)
    for step in range(NEWTON):
        left = dot(left_of(approx), pivot_right)
        approx = 2.0 * approx - product(left, approx)
    return approx


def place_blocks(place_ref, own_ref, other_ref, rows_ref, blocks):
    size = rows_ref.shape[0] // blocks
    for k in range(blocks):
        source = own_ref if k < blocks // 2 else other_ref
        start = k % (blocks // 2) * size
        target = pl.multiple_of((place_ref[0] ^ k) * size, size)
        rows_ref[pl.ds(target, size), :] = source[start:start + size, :]


def first_kernel(blocks, place_ref, own_ref, other_ref, inverse_ref, lower_ref, rows_ref):
    place_blocks(place_ref, own_ref, other_ref, rows_ref, blocks)
    half = inverse_ref.shape[0]
    lower_ref[...] = rows_ref[half:, :]
    inverse_ref[...] = newton(rows_ref[:half, :])


def second_kernel(
    blocks, place_ref, own_ref, other_ref, inverse_first_ref, lower_ref, inverse_ref, upper_ref, rows_ref
):
    place_blocks(place_ref, own_ref, other_ref, rows_ref, blocks)
    half = inverse_ref.shape[0]
    upper = rows_ref[:half, :]
    upper_ref[...] = upper
    lower_factor = product(lower_ref[...], inverse_first_ref[...])
    inverse_ref[...] = newton(rows_ref[half:, :] - product(lower_factor, upper))


def factor_kernel(rows_ref, inverse_first_ref, inverse_second_ref, upper_ref, first_out, second_out):
    half = upper_ref.shape[0]
    first_factor = product(rows_ref[:half, :].T, inverse_first_ref[...])
    updated = rows_ref[half:, :].T - product(first_factor, upper_ref[...])
    first_out[...] = first_factor[:, None, :]
    second_out[...] = product(updated, inverse_second_ref[...])[:, None, :]


def contract(a, b, dims):
    return lax.dot_general(a, b, (dims, ((), ())), preferred_element_type=F32)


def pick_kernel(
    blocks, place_ref, wanted_ref, own_diagonal_ref, coupling_ref, picked_ref, left_ref, right_ref,
    column_ref, chosen_ref,
):
    @pl.when(pl.program_id(0) == 0)
    def _():
        first_column, first_row, me = place_ref[0], place_ref[1], place_ref[2]
        panel, columns = chosen_ref.shape
        share = own_diagonal_ref.shape[1]
        lanes = column_ref.shape[1]
        column_ref[...] = jnp.broadcast_to(wanted_ref[...], (lanes, panel)).astype(F32).T.astype(jnp.int32)
        size = panel // blocks
        half = left_ref.shape[1]
        for k in range(blocks):
            rows = slice(k * size, (k + 1) * size)
            start = pl.multiple_of((me ^ k) * size, size)
            wanted = column_ref[pl.ds(start, size), :][:, :1]
            here = wanted - first_column == lax.broadcasted_iota(jnp.int32, (size, columns), 1)
            chosen_ref[rows, :] = jnp.where(here, F32(1.0), F32(0.0)).astype(BF16)
            owned = wanted - first_row == lax.broadcasted_iota(jnp.int32, (size, share), 1)
            entry = jnp.sum(jnp.where(owned, own_diagonal_ref[...], F32(0.0)), axis=1, keepdims=True)
            index = lax.broadcasted_iota(jnp.int32, (size, half), 0) + start
            column = lax.broadcasted_iota(jnp.int32, (size, half), 1)
            left_ref[rows, :] = jnp.where(index == column, entry, F32(0.0))
            right_ref[rows, :] = jnp.where(index == column + half, entry, F32(0.0))

    picked_ref[...] = contract(chosen_ref[...], coupling_ref[...], ((1,), (1,))).astype(BF16)


def pivot_terms(total, keep_ref, send_ref):
    half = keep_ref.shape[0]
    keep_ref[...] = total[:half]
    send_ref[...] = total[half:]


def left_kernel(place_ref, picked_ref, diagonal_ref, *refs):
    *pieces, solves_ref, keep_ref, send_ref = refs
    if len(pieces) == 1:
        solves_ref[...] = pieces[0][...]
    else:
        size = pieces[0].shape[0] // 2
        solves_ref[pl.ds(pl.multiple_of(place_ref[0] * 2 * size, size), 2 * size), :] = pieces[0][...]
        for i, piece in enumerate(pieces[1:]):
            start = pl.multiple_of((place_ref[0] ^ (1 + i // 2)) * 2 * size + i % 2 * size, size)
            solves_ref[pl.ds(start, size), :] = piece[...]
    half = diagonal_ref.shape[1]
    pivot_terms(dot(picked_ref[...], solves_ref[:, :half]) + diagonal_ref[...], keep_ref, send_ref)


def right_kernel(picked_ref, diagonal_ref, solves_ref, keep_ref, send_ref):
    half = diagonal_ref.shape[1]
    pivot_terms(dot(picked_ref[...], solves_ref[:, half:]) + diagonal_ref[...], keep_ref, send_ref)


def schur_kernel(place_ref, coupling_ref, solves_ref, keep_ref, send_ref, turned_ref):
    core = place_ref[1]
    share = keep_ref.shape[1]

    @pl.when(pl.program_id(0) == 0)
    def _():
        turned_ref[...] = solves_ref[...].T

    both = dot(turned_ref[...], coupling_ref[...])
    one, two = both[:, :share], both[:, share:]
    keep_ref[...] = jnp.where(core == 0, one, two)
    send_ref[...] = jnp.where(core == 0, two, one)


def in_vmem(kernel, out_shape, flops, *args, scratch=(), scalars=0, grid=(), in_blocks=None, out_blocks=None, limit=28 << 20, moved=1 << 10):
    vmem = pl.BlockSpec(memory_space=pltpu.VMEM)
    smem = pl.BlockSpec(memory_space=pltpu.SMEM)
    return pl.pallas_call(
        kernel,
        out_shape=out_shape,
        grid=grid,
        in_specs=[smem] * scalars + list(in_blocks or [vmem] * (len(args) - scalars)),
        out_specs=out_blocks or jax.tree.map(lambda _: vmem, out_shape),
        scratch_shapes=scratch,
        compiler_params=pltpu.CompilerParams(vmem_limit_bytes=limit),
        cost_estimate=pl.CostEstimate(flops=flops, bytes_accessed=moved, transcendentals=0),
    )(*args)


def swap(x, axis, bit):
    count = lax.axis_size(axis)
    return lax.ppermute(x, axis, [(i, i ^ bit) for i in range(count)])


def after(x, *others):
    return lax.optimization_barrier((x,) + others)[0]


def bits_of(count):
    return [1 << i for i in range(count.bit_length() - 1)]


def gather_pieces(block, rows, first):
    if rows != 4:
        return [lax.all_gather(block, "row", axis=0, tiled=True)]
    half = block.shape[0] // 2
    upper, lower = block[:half], block[half:]
    lower_x, upper_y = swap(lower, "row", 1), swap(upper, "row", 2)
    upper_x, lower_y = swap(upper, "row", 1), swap(lower, "row", 2)
    upper_far, lower_far = swap(after(upper_y, *first), "row", 1), swap(after(lower_x, *first), "row", 2)
    return [block, upper_x, lower_x, upper_y, lower_y, upper_far, lower_far]


def halved(keep, got):
    half = keep.shape[0] // 2
    goes = keep[half:] + got[half:]
    return keep[:half] + got[:half], goes


def sum_pivots(keep, send, rows, layers):
    got = swap(send, "scen", 1)
    size = keep.shape[0] // rows
    block = lambda x, k: x[k * size:(k + 1) * size]
    arrived = [swap(block(keep, k) + block(got, k), "row", k) for k in range(1, rows)]
    part = sum(arrived, block(keep, 0) + block(got, 0))
    for bit in bits_of(layers):
        part = part + swap(part, "scen", 2 * bit)
    whole = jnp.concatenate([part] + [swap(part, "row", k) for k in range(1, rows)], axis=0)
    return whole, swap(whole, "scen", 1), part


def shards(coupling, solves, border_diagonal, panel_rows):
    half = HALF
    coupling, solves = coupling[0], solves[0]
    local, row_count = coupling.shape
    block, panel = solves.shape
    scen, rows = lax.axis_size("scen"), lax.axis_size("row")
    layers = scen // 2
    row, place = lax.axis_index("row"), lax.axis_index("scen")
    layer, core = place // 2, place % 2
    share = row_count // scen
    base = row * row_count + place * share

    blocks = 2 * rows
    size = panel // blocks
    me = core * rows + row
    corner_shape = jax.ShapeDtypeStruct((panel, half), F32)
    places = jnp.stack([row * row_count, base, me]).astype(jnp.int32)
    corner_shape = jax.ShapeDtypeStruct((panel, half), F32)
    whole = lambda *shape: pl.BlockSpec(shape, lambda i: (0, 0))
    picked, *diagonals = in_vmem(
        functools.partial(pick_kernel, blocks),
        (jax.ShapeDtypeStruct((panel, local), BF16), corner_shape, corner_shape),
        0,
        places, panel_rows[None, :], border_diagonal.T, coupling, scalars=1,
        grid=(STEPS,),
        in_blocks=[whole(1, panel), whole(1, share), pl.BlockSpec((local // STEPS, row_count), lambda i: (i, 0))],
        out_blocks=(pl.BlockSpec((panel, local // STEPS), lambda i: (0, i)), whole(panel, half), whole(panel, half)),
        scratch=[pltpu.VMEM((panel, 128), jnp.int32), pltpu.VMEM((panel, row_count), BF16)], limit=LARGE,
    )
    pieces = gather_pieces(solves, rows, (picked,))

    glob = base + jnp.arange(share, dtype=jnp.int32)
    diag_part = jnp.where(panel_rows[:, None] == glob[None, :], border_diagonal[:, 0][None, :], F32(0.0))

    piece = jax.ShapeDtypeStruct((panel // 2, half), F32)
    gathered = jax.ShapeDtypeStruct((local, panel), BF16)
    cost = 0
    solves_all, keep, send = in_vmem(
        left_kernel, (gathered, piece, piece), cost,
        row.astype(jnp.int32)[None], picked, diagonals[0], *pieces, scalars=1,
    )
    first_own, first_other, first_summed = sum_pivots(keep, send, rows, layers)
    keep, send = in_vmem(right_kernel, (piece, piece), cost, picked, diagonals[1], solves_all)
    second_own, second_other, _ = sum_pivots(keep, send, rows, layers)

    if share % 128:
        terms = contract(solves_all, coupling, ((0,), (0,)))
        part = lax.psum_scatter(terms, "scen", scatter_dimension=1, tiled=True)
    else:
        where = jnp.stack([layer, core]).astype(jnp.int32)
        rowsum = jax.ShapeDtypeStruct((layers * panel, share), F32)

        def relative(i):
            last = layers.bit_length() - 2
            return sum(((i >> b) & 1) << (last - b) for b in range(last + 1)) ^ (lax.axis_index("scen") // 2)

        keep, send = in_vmem(
            schur_kernel, (rowsum, rowsum), 0,
            where, coupling, solves_all, scalars=1,
            grid=(layers,),
            in_blocks=[pl.BlockSpec((local, 2 * share), lambda i: (0, relative(i))), whole(local, panel)],
            out_blocks=(pl.BlockSpec((panel, share), lambda i: (i, 0)),) * 2,
            scratch=[pltpu.VMEM((panel, local), BF16)],
        )
        keep, goes = halved(keep, swap(send, "scen", 1))
        goes = after(goes, first_summed)
        for bit in bits_of(layers)[:-1]:
            keep, goes = halved(keep, swap(goes, "scen", 2 * bit))
        part = keep + swap(goes, "scen", layers)
    own_rows = part + diag_part

    square = jax.ShapeDtypeStruct((half, half), F32)
    scratch = [pltpu.VMEM((panel, half), F32)]
    at = me.astype(jnp.int32)[None]
    inverse_first, lower = in_vmem(
        functools.partial(first_kernel, blocks), (square, square), 2 * 16 * 3 * half**3,
        at, first_own, first_other, scratch=scratch, scalars=1, moved=NEWTON_BYTES,
    )
    inverse_second, upper = in_vmem(
        functools.partial(second_kernel, blocks), (square, square), 2 * 18 * 3 * half**3,
        at, second_own, second_other, inverse_first, lower, scratch=scratch, scalars=1, moved=NEWTON_BYTES,
    )
    out = jax.ShapeDtypeStruct((share, 1, half), F32)
    return in_vmem(
        factor_kernel, (out, out), 2 * 9 * share * half**2, own_rows, inverse_first, inverse_second, upper
    )


def solution(mesh):
    placed = (P("scen", None, "row"), P("scen", "row", None), P("scen", "row"), P())
    return jax.shard_map(
        shards,
        mesh=mesh,
        in_specs=placed,
        out_specs=(P("scen", "row", None), P("scen", "row", None)),
        check_vma=False,
    )
```

time: 80.9 us -> 92 us (1.14)
  waiting for transfers between devices: 18.9 us -> 30.8 us
  Pallas kernels: 17.6 us -> 22.4 us
  starting transfers between devices: 35.8 us -> 31.8 us
  local copies, waits for them, and re-layouts: 5.76 us -> 4.56 us
    ppermute x27 -> x29, waiting for transfers between devices: 18.9 us -> 30.8 us  [swap(): return lax.ppermute(x, axis, [(i, i ^ bit) for i in range(count)])]
    pallas_call x7, Pallas kernels: 17.6 us -> 22.4 us  [in_vmem(): pl.pallas_call(kernel, out_shape=out_shape, grid=grid, in_specs=[smem] *...]
    ppermute x27 -> x29, starting transfers between devices: 35.8 us -> 31.8 us  [swap(): return lax.ppermute(x, axis, [(i, i ^ bit) for i in range(count)])]
    dynamic_slice x1 -> x0, local copies, waits for them, and re-layouts: 1.05 us -> none  [shards(): lax.dynamic_slice_in_dim(panel_rows, (me ^ k) * size, size, 0)]
    add x8 -> x6, other arithmetic: 1.24 us -> 0.23 us  [the longest x1 0.11 us: halved(): return (keep[:half] + got[:half], goes)]
  transfers between devices with their start and end apart: 27 -> 29, of which waited for: 12 -> 14; matrix products, arithmetic and copies ran while one was open for 3% -> 1% of each run, Pallas kernels for 20% -> 22%
where the time goes in v1:
time: 92 us; the launch traced here: 91.7 us
  starting transfers between devices  31.8 us (35%)
  waiting for transfers between devices  30.8 us (33%)
  Pallas kernels  22.4 us (24%)
  local copies, waits for them, and re-layouts  4.56 us (5%)
  other arithmetic  1.19 us (1%)
    ppermute x29, starting transfers between devices, swap(): return lax.ppermute(x, axis, [(i, i ^ bit) for i in range(count)])  31.8 us
    ppermute x29, waiting for transfers between devices, swap(): return lax.ppermute(x, axis, [(i, i ^ bit) for i in range(count)])  30.8 us
    pallas_call x7, Pallas kernels, in_vmem(): pl.pallas_call(kernel, out_shape=out_shape, grid=grid, in_specs=[smem] *...  22.4 us
    unnamed x14, local copies, waits for them, and re-layouts  3.51 us
  transfers between devices with their start and end apart: 29, of which 14 were waited for; matrix products, arithmetic and copies ran while one was open for 1% of the time, Pallas kernels for 22%

profile of v1, /device:TPU:0, one launch (start us, length us, event | category | flops | bytes accessed | tf_op | source)
XLA Modules:
  0.0 91.7 jit_solution(886302593396336582)
XLA Ops:
  0.6 1.1 %slice_bitcast_fusion = (bf16[192,512]{1,0:T(8,128)(2,1)S(1)}, bf16[192,512]{1,0:T(8,128)(2,1)S(1)}) fusion(bf16[1,384,512]{2,1,0:T(8,128)(2,1)} %param.5), kind=kLoop, calls=%fused_computation.8 | loop fusion | bytes 786432 | tf_op jit(solution)/shard_map/slice | solution.py:194
  1.7 3.0 %collective-permute-start.1 = (bf16[192,512]{1,0:T(8,128)(2,1)S(1)}, bf16[192,512]{1,0:T(8,128)(2,1)S(1)}, u32[]{:S(2)}, u32[]{:S(2)}) collective-permute-start(bf16[192,512]{1,0:T(8,128)(2,1)S(1)} %get-tuple-element.44), channel_id=1, source_target_pairs={{0,1},{1,0},{2,3},{3,2},{4,5},{5,4},{6,7},{7,6},{8,9},{9,8},{10,11... | collective-permute-start | bytes 589832 | tf_op jit(solution)/shard_map/ppermute | solution.py:179
  4.7 1.5 %collective-permute-start.2 = (bf16[192,512]{1,0:T(8,128)(2,1)S(1)}, bf16[192,512]{1,0:T(8,128)(2,1)S(1)}, u32[]{:S(2)}, u32[]{:S(2)}) collective-permute-start(bf16[192,512]{1,0:T(8,128)(2,1)S(1)} %get-tuple-element.45), channel_id=1, source_target_pairs={{0,2},{1,3},{2,0},{3,1},{4,6},{5,7},{6,4},{7,5},{8,10},{9,11},{10,... | collective-permute-start | bytes 589832 | tf_op jit(solution)/shard_map/ppermute | solution.py:179
  6.2 0.5 collective-permute-start.3
  6.7 0.1 collective-permute-start
  6.8 0.7 pad_add_fusion.1.place_ref
  7.5 6.8 %shard_map.59 = (bf16[512,1536]{1,0:T(8,128)(2,1)}, f32[512,256]{1,0:T(8,128)}, f32[512,256]{1,0:T(8,128)}) custom-call(s32[3]{0:T(128)} %pad_add_fusion.1.place_ref, s32[1,512]{1,0:T(1,128)} %bitcast.18, f32[1,128]{1,0:T(1,128)} %bitcast.19, bf16[1536,1024]{1,0:T(8,128)(2,1)} %bitcast.15), custom_call_target="tpu_custom_call" | custom-call | bytes 1024 | tf_op jit(solution)/shard_map/pallas_call | solution.py:165
  14.3 0.0 collective-permute-done.1.refs_2_
  14.3 0.0 collective-permute-done.2.refs_3_
  14.3 2.0 %collective-permute-start.4 = (bf16[192,512]{1,0:T(8,128)(2,1)S(1)}, bf16[192,512]{1,0:T(8,128)(2,1)S(1)}, u32[]{:S(2)}, u32[]{:S(2)}) collective-permute-start(bf16[192,512]{1,0:T(8,128)(2,1)S(1)} %collective-permute-done.2.refs_3_), channel_id=1, source_target_pairs={{0,1},{1,0},{2,3},{3,2},{4,5},{5,4},{6,7},{7,6},{8,9},{9,8},{10,11... | collective-permute-start | bytes 589832 | tf_op jit(solution)/shard_map/ppermute | solution.py:179
  16.3 1.5 %collective-permute-start.5 = (bf16[192,512]{1,0:T(8,128)(2,1)S(1)}, bf16[192,512]{1,0:T(8,128)(2,1)S(1)}, u32[]{:S(2)}, u32[]{:S(2)}) collective-permute-start(bf16[192,512]{1,0:T(8,128)(2,1)S(1)} %collective-permute-done.1.refs_2_), channel_id=1, source_target_pairs={{0,2},{1,3},{2,0},{3,1},{4,6},{5,7},{6,4},{7,5},{8,10},{9,11},{10,... | collective-permute-start | bytes 589832 | tf_op jit(solution)/shard_map/ppermute | solution.py:179
  17.8 2.3 %collective-permute-done.4.refs_5_ = bf16[192,512]{1,0:T(8,128)(2,1)S(1)} collective-permute-done((bf16[192,512]{1,0:T(8,128)(2,1)S(1)}, bf16[192,512]{1,0:T(8,128)(2,1)S(1)}, u32[]{:S(2)}, u32[]{:S(2)}) %collective-permute-start.4) | collective-permute-done | bytes 196640 | tf_op jit(solution)/shard_map/ppermute | solution.py:179
  20.1 1.8 %collective-permute-done.5.refs_6_ = bf16[192,512]{1,0:T(8,128)(2,1)S(1)} collective-permute-done((bf16[192,512]{1,0:T(8,128)(2,1)S(1)}, bf16[192,512]{1,0:T(8,128)(2,1)S(1)}, u32[]{:S(2)}, u32[]{:S(2)}) %collective-permute-start.5) | collective-permute-done | bytes 196640 | tf_op jit(solution)/shard_map/ppermute | solution.py:179
  22.0 1.4 %copy-done.1 = bf16[512,1536]{1,0:T(8,128)(2,1)S(1)} copy-done((bf16[512,1536]{1,0:T(8,128)(2,1)S(1)}, bf16[512,1536]{1,0:T(8,128)(2,1)}, u32[]{:S(2)}) %copy-start.1) | copy-done | bytes 1572888
  23.4 1.0 %copy-done.4 = f32[512,256]{1,0:T(8,128)S(1)} copy-done((f32[512,256]{1,0:T(8,128)S(1)}, f32[512,256]{1,0:T(8,128)}, u32[]{:S(2)}) %copy-start.4) | copy-done | bytes 524312
  24.4 0.7 shard_map.60
  25.1 0.1 collective-permute-start.7
  25.2 0.1 pad_add_fusion.place_ref
  25.3 1.0 %copy-done = bf16[1,1536,1024]{2,1,0:T(8,128)(2,1)S(1)} copy-done((bf16[1,1536,1024]{2,1,0:T(8,128)(2,1)S(1)}, bf16[1,1536,1024]{2,1,0:T(8,128)(2,1)}, u32[]{:S(2)}) %copy-start) | copy-done | bytes 3145752
  26.3 3.8 %shard_map.61 = (f32[2048,128]{1,0:T(8,128)S(1)}, f32[2048,128]{1,0:T(8,128)S(1)}) custom-call(s32[2]{0:T(128)S(1)} %pad_add_fusion.place_ref, bf16[1536,1024]{1,0:T(8,128)(2,1)S(1)} %bitcast.16, bf16[1536,512]{1,0:T(8,128)(2,1)S(1)} %get-tuple-element.23.solves_ref), custom_call_target="tpu_custom_call" | custom-call | bytes 1024 | tf_op jit(solution)/shard_map/pallas_call | solution.py:165
  30.1 0.1 collective-permute-start.6
  30.2 0.0 collective-permute-done.7
  30.2 0.1 collective-permute-start.8
  30.4 2.9 %collective-permute-start.10 = (f32[64,256]{1,0:T(8,128)S(1)}, f32[64,256]{1,0:T(8,128)S(1)}, u32[]{:S(2)}, u32[]{:S(2)}) collective-permute-start(f32[64,256]{1,0:T(8,128)S(1)} %get-tuple-element.42), channel_id=1, source_target_pairs={{0,3},{1,2},{2,1},{3,0},{4,7},{5,6},{6,5},{7,4},{8,11},{9,10},{10,... | collective-permute-start | bytes 196616 | tf_op jit(solution)/shard_map/ppermute | solution.py:179
  33.3 0.5 collective-permute-start.9
  33.8 0.6 shard_map.63
  34.4 0.1 collective-permute-start.19
  34.4 0.6 collective-permute-done.8
  35.0 2.2 %collective-permute-done.10 = f32[64,256]{1,0:T(8,128)S(1)} collective-permute-done((f32[64,256]{1,0:T(8,128)S(1)}, f32[64,256]{1,0:T(8,128)S(1)}, u32[]{:S(2)}, u32[]{:S(2)}) %collective-permute-start.10) | collective-permute-done | bytes 65568 | tf_op jit(solution)/shard_map/ppermute | solution.py:179
  37.2 1.1 %collective-permute-done.9 = f32[64,256]{1,0:T(8,128)S(1)} collective-permute-done((f32[64,256]{1,0:T(8,128)S(1)}, f32[64,256]{1,0:T(8,128)S(1)}, u32[]{:S(2)}, u32[]{:S(2)}) %collective-permute-start.9) | collective-permute-done | bytes 65568 | tf_op jit(solution)/shard_map/ppermute | solution.py:179
  38.4 1.6 %collective-permute-start.11 = (f32[64,256]{1,0:T(8,128)S(1)}, f32[64,256]{1,0:T(8,128)S(1)}, u32[]{:S(2)}, u32[]{:S(2)}) collective-permute-start(f32[64,256]{1,0:T(8,128)S(1)} %fusion.7), channel_id=1, source_target_pairs={{0,8},{4,12},{8,0},{12,4},{16,24},{20,28},{24,16},{28,20},{1,9},{5... | collective-permute-start | bytes 196616 | tf_op jit(solution)/shard_map/ppermute | solution.py:179
  40.0 2.7 %collective-permute-done.11 = f32[64,256]{1,0:T(8,128)S(1)} collective-permute-done((f32[64,256]{1,0:T(8,128)S(1)}, f32[64,256]{1,0:T(8,128)S(1)}, u32[]{:S(2)}, u32[]{:S(2)}) %collective-permute-start.11) | collective-permute-done | bytes 65568 | tf_op jit(solution)/shard_map/ppermute | solution.py:179
  42.7 2.6 %collective-permute-start.12 = (f32[64,256]{1,0:T(8,128)S(1)}, f32[64,256]{1,0:T(8,128)S(1)}, u32[]{:S(2)}, u32[]{:S(2)}) collective-permute-start(f32[64,256]{1,0:T(8,128)S(1)} %add.105), channel_id=1, source_target_pairs={{0,16},{4,20},{8,24},{12,28},{16,0},{20,4},{24,8},{28,12},{1,17},{... | collective-permute-start | bytes 196616 | tf_op jit(solution)/shard_map/ppermute | solution.py:179
  45.4 0.7 collective-permute-start.20
  46.1 1.5 %collective-permute-start.22 = (f32[64,256]{1,0:T(8,128)S(1)}, f32[64,256]{1,0:T(8,128)S(1)}, u32[]{:S(2)}, u32[]{:S(2)}) collective-permute-start(f32[64,256]{1,0:T(8,128)S(1)} %get-tuple-element.39), channel_id=1, source_target_pairs={{0,3},{1,2},{2,1},{3,0},{4,7},{5,6},{6,5},{7,4},{8,11},{9,10},{10,... | collective-permute-start | bytes 196616 | tf_op jit(solution)/shard_map/ppermute | solution.py:179
  47.5 1.4 %collective-permute-start.21 = (f32[64,256]{1,0:T(8,128)S(1)}, f32[64,256]{1,0:T(8,128)S(1)}, u32[]{:S(2)}, u32[]{:S(2)}) collective-permute-start(f32[64,256]{1,0:T(8,128)S(1)} %get-tuple-element.40), channel_id=1, source_target_pairs={{0,2},{1,3},{2,0},{3,1},{4,6},{5,7},{6,4},{7,5},{8,10},{9,11},{10,... | collective-permute-start | bytes 196616 | tf_op jit(solution)/shard_map/ppermute | solution.py:179
  49.0 0.0 collective-permute-done.12
  49.0 0.0 collective-permute-done.6
  49.0 0.1 slice_add_fusion.1
  49.1 1.6 %collective-permute-start.13 = (f32[1024,128]{1,0:T(8,128)S(1)}, f32[1024,128]{1,0:T(8,128)S(1)}, u32[]{:S(2)}, u32[]{:S(2)}) collective-permute-start(f32[1024,128]{1,0:T(8,128)S(1)} %get-tuple-element.28), channel_id=1, source_target_pairs={{0,8},{4,12},{8,0},{12,4},{16,24},{20,28},{24,16},{28,20},{1,9},{5... | collective-permute-start | bytes 1572872 | tf_op jit(solution)/shard_map/ppermute | solution.py:179
  50.8 0.5 collective-permute-done.22
  51.2 0.7 collective-permute-done.21
  52.0 1.6 %collective-permute-start.23 = (f32[64,256]{1,0:T(8,128)S(1)}, f32[64,256]{1,0:T(8,128)S(1)}, u32[]{:S(2)}, u32[]{:S(2)}) collective-permute-start(f32[64,256]{1,0:T(8,128)S(1)} %fusion.4), channel_id=1, source_target_pairs={{0,8},{4,12},{8,0},{12,4},{16,24},{20,28},{24,16},{28,20},{1,9},{5... | collective-permute-start | bytes 196616 | tf_op jit(solution)/shard_map/ppermute | solution.py:179
  53.6 8.4 %collective-permute-done.23 = f32[64,256]{1,0:T(8,128)S(1)} collective-permute-done((f32[64,256]{1,0:T(8,128)S(1)}, f32[64,256]{1,0:T(8,128)S(1)}, u32[]{:S(2)}, u32[]{:S(2)}) %collective-permute-start.23) | collective-permute-done | bytes 65568 | tf_op jit(solution)/shard_map/ppermute | solution.py:179
  62.0 2.1 %collective-permute-start.24 = (f32[64,256]{1,0:T(8,128)S(1)}, f32[64,256]{1,0:T(8,128)S(1)}, u32[]{:S(2)}, u32[]{:S(2)}) collective-permute-start(f32[64,256]{1,0:T(8,128)S(1)} %add.120), channel_id=1, source_target_pairs={{0,16},{4,20},{8,24},{12,28},{16,0},{20,4},{24,8},{28,12},{1,17},{... | collective-permute-start | bytes 196616 | tf_op jit(solution)/shard_map/ppermute | solution.py:179
  64.1 2.0 %collective-permute-start.16 = (f32[64,256]{1,0:T(8,128)S(1)}, f32[64,256]{1,0:T(8,128)S(1)}, u32[]{:S(2)}, u32[]{:S(2)}) collective-permute-start(f32[64,256]{1,0:T(8,128)S(1)} %add.106), channel_id=1, source_target_pairs={{0,2},{1,3},{2,0},{3,1},{4,6},{5,7},{6,4},{7,5},{8,10},{9,11},{10,... | collective-permute-start | bytes 196616 | tf_op jit(solution)/shard_map/ppermute | solution.py:179
  66.2 1.4 %collective-permute-start.15 = (f32[64,256]{1,0:T(8,128)S(1)}, f32[64,256]{1,0:T(8,128)S(1)}, u32[]{:S(2)}, u32[]{:S(2)}) collective-permute-start(f32[64,256]{1,0:T(8,128)S(1)} %add.106), channel_id=1, source_target_pairs={{0,1},{1,0},{2,3},{3,2},{4,5},{5,4},{6,7},{7,6},{8,9},{9,8},{10,11... | collective-permute-start | bytes 196616 | tf_op jit(solution)/shard_map/ppermute | solution.py:179
  67.6 0.2 collective-permute-start.27
  67.8 2.0 %collective-permute-done.17 = f32[64,256]{1,0:T(8,128)S(1)} collective-permute-done((f32[64,256]{1,0:T(8,128)S(1)}, f32[64,256]{1,0:T(8,128)S(1)}, u32[]{:S(2)}, u32[]{:S(2)}) %collective-permute-start.17) | collective-permute-done | bytes 65568 | tf_op jit(solution)/shard_map/ppermute | solution.py:179
  69.9 0.7 collective-permute-start.26
  70.5 0.7 collective-permute-start.25
  71.2 0.1 collective-permute-start.18
  71.3 1.6 %collective-permute-done.27 = f32[64,256]{1,0:T(8,128)S(1)} collective-permute-done((f32[64,256]{1,0:T(8,128)S(1)}, f32[64,256]{1,0:T(8,128)S(1)}, u32[]{:S(2)}, u32[]{:S(2)}) %collective-permute-start.27) | collective-permute-done | bytes 65568 | tf_op jit(solution)/shard_map/ppermute | solution.py:179
  72.9 1.2 %collective-permute-done.26 = f32[64,256]{1,0:T(8,128)S(1)} collective-permute-done((f32[64,256]{1,0:T(8,128)S(1)}, f32[64,256]{1,0:T(8,128)S(1)}, u32[]{:S(2)}, u32[]{:S(2)}) %collective-permute-start.26) | collective-permute-done | bytes 65568 | tf_op jit(solution)/shard_map/ppermute | solution.py:179
  74.1 0.7 collective-permute-done.25
  74.8 0.1 collective-permute-start.28
  74.9 1.0 %collective-permute-start.14 = (f32[512,128]{1,0:T(8,128)S(1)}, f32[512,128]{1,0:T(8,128)S(1)}, u32[]{:S(2)}, u32[]{:S(2)}) collective-permute-start(f32[512,128]{1,0:T(8,128)S(1)} %slice_add_fusion.2), channel_id=1, source_target_pairs={{0,16},{4,20},{8,24},{12,28},{16,0},{20,4},{24,8},{28,12},{1,17},{... | collective-permute-start | bytes 786440 | tf_op jit(solution)/shard_map/ppermute | solution.py:179
  76.0 4.3 %shard_map.62 = (f32[256,256]{1,0:T(8,128)S(1)}, f32[256,256]{1,0:T(8,128)S(1)}) custom-call(s32[1]{0:T(128)} %bitcast.6.place_ref, f32[256,256]{1,0:T(8,128)S(1)} %pad_maximum_fusion.own_ref, f32[256,256]{1,0:T(8,128)S(1)} %collective-permute-done.18.other_ref), custom_call_target="tpu_custom_call" | custom-call | flops 1610612736 | bytes 16777216 | tf_op jit(solution)/shard_map/pallas_call | solution.py:165
  80.3 0.0 copy-start.5
  80.3 0.0 copy-start.6
  80.4 4.9 %shard_map.64 = (f32[256,256]{1,0:T(8,128)S(1)}, f32[256,256]{1,0:T(8,128)S(1)}) custom-call(s32[1]{0:T(128)} %bitcast.6.place_ref, f32[256,256]{1,0:T(8,128)S(1)} %pad_maximum_fusion.1.own_ref, f32[256,256]{1,0:T(8,128)S(1)} %collective-permute-done.28.other_ref, f32[256,256]{1,0:T(8,128)S(1)} %get-tuple-element.29.inverse_first_ref, ...), custom_call_target="tpu_custom_call" | custom-call | flops 1811939328 | bytes 16777216 | tf_op jit(solution)/shard_map/pallas_call | solution.py:165
  85.3 4.9 %collective-permute-done.14 = f32[512,128]{1,0:T(8,128)S(1)} collective-permute-done((f32[512,128]{1,0:T(8,128)S(1)}, f32[512,128]{1,0:T(8,128)S(1)}, u32[]{:S(2)}, u32[]{:S(2)}) %collective-permute-start.14) | collective-permute-done | bytes 262176 | tf_op jit(solution)/shard_map/ppermute | solution.py:179
  90.2 0.1 fusion.1.rows_ref
  90.3 1.3 %shard_map.65 = (f32[128,1,256]{2,1,0:T(1,128)}, f32[128,1,256]{2,1,0:T(1,128)}) custom-call(f32[512,128]{1,0:T(8,128)S(1)} %fusion.1.rows_ref, f32[256,256]{1,0:T(8,128)S(1)} %get-tuple-element.29.inverse_first_ref, f32[256,256]{1,0:T(8,128)S(1)} %get-tuple-element.34.inverse_second_ref, f32[256,256]{1,0:T(8,128)S(1)} %get-tuple-element.35.upper_ref), custom_call_target="tpu_custom_call" | custom-call | flops 150994944 | bytes 1024 | tf_op jit(solution)/shard_map/pallas_call | solution.py:165
  (32 shorter events, 0.2 us)
Async XLA Ops:
  1.7 12.6 %collective-permute-start.1 = (bf16[192,512]{1,0:T(8,128)(2,1)S(1)}, bf16[192,512]{1,0:T(8,128)(2,1)S(1)}, u32[]{:S(2)}, u32[]{:S(2)}) collective-permute-start(bf16[192,512]{1,0:T(8,128)(2,1)S(1)} %get-tuple-element.44), channel_id=1, source_target_pairs={{0,1},{1,0},{2,3},{3,2},{4,5},{5,4},{6,7},{7,6},{8,9},{9,8},{10,11... | collective-permute-start | bytes 589832 | tf_op jit(solution)/shard_map/ppermute | solution.py:179
  4.7 9.6 %collective-permute-start.2 = (bf16[192,512]{1,0:T(8,128)(2,1)S(1)}, bf16[192,512]{1,0:T(8,128)(2,1)S(1)}, u32[]{:S(2)}, u32[]{:S(2)}) collective-permute-start(bf16[192,512]{1,0:T(8,128)(2,1)S(1)} %get-tuple-element.45), channel_id=1, source_target_pairs={{0,2},{1,3},{2,0},{3,1},{4,6},{5,7},{6,4},{7,5},{8,10},{9,11},{10,... | collective-permute-start | bytes 589832 | tf_op jit(solution)/shard_map/ppermute | solution.py:179
  6.2 11.6 %collective-permute-start.3 = (bf16[192,512]{1,0:T(8,128)(2,1)S(1)}, bf16[192,512]{1,0:T(8,128)(2,1)S(1)}, u32[]{:S(2)}, u32[]{:S(2)}) collective-permute-start(bf16[192,512]{1,0:T(8,128)(2,1)S(1)} %get-tuple-element.44), channel_id=1, source_target_pairs={{0,2},{1,3},{2,0},{3,1},{4,6},{5,7},{6,4},{7,5},{8,10},{9,11},{10,... | collective-permute-start | bytes 589832 | tf_op jit(solution)/shard_map/ppermute | solution.py:179
  6.7 11.1 %collective-permute-start = (bf16[192,512]{1,0:T(8,128)(2,1)S(1)}, bf16[192,512]{1,0:T(8,128)(2,1)S(1)}, u32[]{:S(2)}, u32[]{:S(2)}) collective-permute-start(bf16[192,512]{1,0:T(8,128)(2,1)S(1)} %get-tuple-element.45), channel_id=1, source_target_pairs={{0,1},{1,0},{2,3},{3,2},{4,5},{5,4},{6,7},{7,6},{8,9},{9,8},{10,11... | collective-permute-start | bytes 589832 | tf_op jit(solution)/shard_map/ppermute | solution.py:179
  7.5 14.5 %copy-start.2 = (bf16[1,384,512]{2,1,0:T(8,128)(2,1)S(1)}, bf16[1,384,512]{2,1,0:T(8,128)(2,1)}, u32[]{:S(2)}) copy-start(bf16[1,384,512]{2,1,0:T(8,128)(2,1)} %param.5) | copy-start | bytes 1179652
  14.3 5.9 %collective-permute-start.4 = (bf16[192,512]{1,0:T(8,128)(2,1)S(1)}, bf16[192,512]{1,0:T(8,128)(2,1)S(1)}, u32[]{:S(2)}, u32[]{:S(2)}) collective-permute-start(bf16[192,512]{1,0:T(8,128)(2,1)S(1)} %collective-permute-done.2.refs_3_), channel_id=1, source_target_pairs={{0,1},{1,0},{2,3},{3,2},{4,5},{5,4},{6,7},{7,6},{8,9},{9,8},{10,11... | collective-permute-start | bytes 589832 | tf_op jit(solution)/shard_map/ppermute | solution.py:179
  16.3 5.7 %collective-permute-start.5 = (bf16[192,512]{1,0:T(8,128)(2,1)S(1)}, bf16[192,512]{1,0:T(8,128)(2,1)S(1)}, u32[]{:S(2)}, u32[]{:S(2)}) collective-permute-start(bf16[192,512]{1,0:T(8,128)(2,1)S(1)} %collective-permute-done.1.refs_2_), channel_id=1, source_target_pairs={{0,2},{1,3},{2,0},{3,1},{4,6},{5,7},{6,4},{7,5},{8,10},{9,11},{10,... | collective-permute-start | bytes 589832 | tf_op jit(solution)/shard_map/ppermute | solution.py:179
  22.0 1.4 %copy-start.1 = (bf16[512,1536]{1,0:T(8,128)(2,1)S(1)}, bf16[512,1536]{1,0:T(8,128)(2,1)}, u32[]{:S(2)}) copy-start(bf16[512,1536]{1,0:T(8,128)(2,1)} %get-tuple-element.19.picked_ref) | copy-start | bytes 4718596
  23.4 1.0 %copy-start.4 = (f32[512,256]{1,0:T(8,128)S(1)}, f32[512,256]{1,0:T(8,128)}, u32[]{:S(2)}) copy-start(f32[512,256]{1,0:T(8,128)} %get-tuple-element.20.diagonal_ref) | copy-start | bytes 1572868
  24.4 1.9 %copy-start = (bf16[1,1536,1024]{2,1,0:T(8,128)(2,1)S(1)}, bf16[1,1536,1024]{2,1,0:T(8,128)(2,1)}, u32[]{:S(2)}) copy-start(bf16[1,1536,1024]{2,1,0:T(8,128)(2,1)} %param.4) | copy-start | bytes 9437188
  25.1 5.1 %collective-permute-start.7 = (f32[256,256]{1,0:T(8,128)S(1)}, f32[256,256]{1,0:T(8,128)S(1)}, u32[]{:S(2)}, u32[]{:S(2)}) collective-permute-start(f32[256,256]{1,0:T(8,128)S(1)} %get-tuple-element.27), channel_id=1, source_target_pairs={{0,4},{4,0},{8,12},{12,8},{16,20},{20,16},{24,28},{28,24},{1,5},{5... | collective-permute-start | bytes 786440 | tf_op jit(solution)/shard_map/ppermute | solution.py:179
  26.3 7.5 %copy-start.3 = (f32[512,256]{1,0:T(8,128)S(1)}, f32[512,256]{1,0:T(8,128)}, u32[]{:S(2)}) copy-start(f32[512,256]{1,0:T(8,128)} %get-tuple-element.30.diagonal_ref) | copy-start | bytes 1572868
  30.1 18.9 %collective-permute-start.6 = (f32[2048,128]{1,0:T(8,128)S(1)}, f32[2048,128]{1,0:T(8,128)S(1)}, u32[]{:S(2)}, u32[]{:S(2)}) collective-permute-start(f32[2048,128]{1,0:T(8,128)S(1)} %get-tuple-element.25), channel_id=1, source_target_pairs={{0,4},{4,0},{8,12},{12,8},{16,20},{20,16},{24,28},{28,24},{1,5},{5... | collective-permute-start | bytes 3145736 | tf_op jit(solution)/shard_map/ppermute | solution.py:179
  30.2 4.8 %collective-permute-start.8 = (f32[64,256]{1,0:T(8,128)S(1)}, f32[64,256]{1,0:T(8,128)S(1)}, u32[]{:S(2)}, u32[]{:S(2)}) collective-permute-start(f32[64,256]{1,0:T(8,128)S(1)} %get-tuple-element.41), channel_id=1, source_target_pairs={{0,1},{1,0},{2,3},{3,2},{4,5},{5,4},{6,7},{7,6},{8,9},{9,8},{10,11... | collective-permute-start | bytes 196616 | tf_op jit(solution)/shard_map/ppermute | solution.py:179
  30.4 6.9 %collective-permute-start.10 = (f32[64,256]{1,0:T(8,128)S(1)}, f32[64,256]{1,0:T(8,128)S(1)}, u32[]{:S(2)}, u32[]{:S(2)}) collective-permute-start(f32[64,256]{1,0:T(8,128)S(1)} %get-tuple-element.42), channel_id=1, source_target_pairs={{0,3},{1,2},{2,1},{3,0},{4,7},{5,6},{6,5},{7,4},{8,11},{9,10},{10,... | collective-permute-start | bytes 196616 | tf_op jit(solution)/shard_map/ppermute | solution.py:179
  33.3 5.1 %collective-permute-start.9 = (f32[64,256]{1,0:T(8,128)S(1)}, f32[64,256]{1,0:T(8,128)S(1)}, u32[]{:S(2)}, u32[]{:S(2)}) collective-permute-start(f32[64,256]{1,0:T(8,128)S(1)} %get-tuple-element.43), channel_id=1, source_target_pairs={{0,2},{1,3},{2,0},{3,1},{4,6},{5,7},{6,4},{7,5},{8,10},{9,11},{10,... | collective-permute-start | bytes 196616 | tf_op jit(solution)/shard_map/ppermute | solution.py:179
  34.4 11.0 %collective-permute-start.19 = (f32[256,256]{1,0:T(8,128)S(1)}, f32[256,256]{1,0:T(8,128)S(1)}, u32[]{:S(2)}, u32[]{:S(2)}) collective-permute-start(f32[256,256]{1,0:T(8,128)S(1)} %get-tuple-element.32), channel_id=1, source_target_pairs={{0,4},{4,0},{8,12},{12,8},{16,20},{20,16},{24,28},{28,24},{1,5},{5... | collective-permute-start | bytes 786440 | tf_op jit(solution)/shard_map/ppermute | solution.py:179
  38.4 4.3 %collective-permute-start.11 = (f32[64,256]{1,0:T(8,128)S(1)}, f32[64,256]{1,0:T(8,128)S(1)}, u32[]{:S(2)}, u32[]{:S(2)}) collective-permute-start(f32[64,256]{1,0:T(8,128)S(1)} %fusion.7), channel_id=1, source_target_pairs={{0,8},{4,12},{8,0},{12,4},{16,24},{20,28},{24,16},{28,20},{1,9},{5... | collective-permute-start | bytes 196616 | tf_op jit(solution)/shard_map/ppermute | solution.py:179
  42.7 6.2 %collective-permute-start.12 = (f32[64,256]{1,0:T(8,128)S(1)}, f32[64,256]{1,0:T(8,128)S(1)}, u32[]{:S(2)}, u32[]{:S(2)}) collective-permute-start(f32[64,256]{1,0:T(8,128)S(1)} %add.105), channel_id=1, source_target_pairs={{0,16},{4,20},{8,24},{12,28},{16,0},{20,4},{24,8},{28,12},{1,17},{... | collective-permute-start | bytes 196616 | tf_op jit(solution)/shard_map/ppermute | solution.py:179
  45.4 5.3 %collective-permute-start.20 = (f32[64,256]{1,0:T(8,128)S(1)}, f32[64,256]{1,0:T(8,128)S(1)}, u32[]{:S(2)}, u32[]{:S(2)}) collective-permute-start(f32[64,256]{1,0:T(8,128)S(1)} %get-tuple-element.38), channel_id=1, source_target_pairs={{0,1},{1,0},{2,3},{3,2},{4,5},{5,4},{6,7},{7,6},{8,9},{9,8},{10,11... | collective-permute-start | bytes 196616 | tf_op jit(solution)/shard_map/ppermute | solution.py:179
  46.1 5.2 %collective-permute-start.22 = (f32[64,256]{1,0:T(8,128)S(1)}, f32[64,256]{1,0:T(8,128)S(1)}, u32[]{:S(2)}, u32[]{:S(2)}) collective-permute-start(f32[64,256]{1,0:T(8,128)S(1)} %get-tuple-element.39), channel_id=1, source_target_pairs={{0,3},{1,2},{2,1},{3,0},{4,7},{5,6},{6,5},{7,4},{8,11},{9,10},{10,... | collective-permute-start | bytes 196616 | tf_op jit(solution)/shard_map/ppermute | solution.py:179
  47.5 4.4 %collective-permute-start.21 = (f32[64,256]{1,0:T(8,128)S(1)}, f32[64,256]{1,0:T(8,128)S(1)}, u32[]{:S(2)}, u32[]{:S(2)}) collective-permute-start(f32[64,256]{1,0:T(8,128)S(1)} %get-tuple-element.40), channel_id=1, source_target_pairs={{0,2},{1,3},{2,0},{3,1},{4,6},{5,7},{6,4},{7,5},{8,10},{9,11},{10,... | collective-permute-start | bytes 196616 | tf_op jit(solution)/shard_map/ppermute | solution.py:179
  49.1 25.8 %collective-permute-start.13 = (f32[1024,128]{1,0:T(8,128)S(1)}, f32[1024,128]{1,0:T(8,128)S(1)}, u32[]{:S(2)}, u32[]{:S(2)}) collective-permute-start(f32[1024,128]{1,0:T(8,128)S(1)} %get-tuple-element.28), channel_id=1, source_target_pairs={{0,8},{4,12},{8,0},{12,4},{16,24},{20,28},{24,16},{28,20},{1,9},{5... | collective-permute-start | bytes 1572872 | tf_op jit(solution)/shard_map/ppermute | solution.py:179
  52.0 10.0 %collective-permute-start.23 = (f32[64,256]{1,0:T(8,128)S(1)}, f32[64,256]{1,0:T(8,128)S(1)}, u32[]{:S(2)}, u32[]{:S(2)}) collective-permute-start(f32[64,256]{1,0:T(8,128)S(1)} %fusion.4), channel_id=1, source_target_pairs={{0,8},{4,12},{8,0},{12,4},{16,24},{20,28},{24,16},{28,20},{1,9},{5... | collective-permute-start | bytes 196616 | tf_op jit(solution)/shard_map/ppermute | solution.py:179
  62.0 5.6 %collective-permute-start.24 = (f32[64,256]{1,0:T(8,128)S(1)}, f32[64,256]{1,0:T(8,128)S(1)}, u32[]{:S(2)}, u32[]{:S(2)}) collective-permute-start(f32[64,256]{1,0:T(8,128)S(1)} %add.120), channel_id=1, source_target_pairs={{0,16},{4,20},{8,24},{12,28},{16,0},{20,4},{24,8},{28,12},{1,17},{... | collective-permute-start | bytes 196616 | tf_op jit(solution)/shard_map/ppermute | solution.py:179
  64.1 5.7 %collective-permute-start.17 = (f32[64,256]{1,0:T(8,128)S(1)}, f32[64,256]{1,0:T(8,128)S(1)}, u32[]{:S(2)}, u32[]{:S(2)}) collective-permute-start(f32[64,256]{1,0:T(8,128)S(1)} %add.106), channel_id=1, source_target_pairs={{0,3},{1,2},{2,1},{3,0},{4,7},{5,6},{6,5},{7,4},{8,11},{9,10},{10,... | collective-permute-start | bytes 196616 | tf_op jit(solution)/shard_map/ppermute | solution.py:179
  64.1 6.4 %collective-permute-start.16 = (f32[64,256]{1,0:T(8,128)S(1)}, f32[64,256]{1,0:T(8,128)S(1)}, u32[]{:S(2)}, u32[]{:S(2)}) collective-permute-start(f32[64,256]{1,0:T(8,128)S(1)} %add.106), channel_id=1, source_target_pairs={{0,2},{1,3},{2,0},{3,1},{4,6},{5,7},{6,4},{7,5},{8,10},{9,11},{10,... | collective-permute-start | bytes 196616 | tf_op jit(solution)/shard_map/ppermute | solution.py:179
  66.2 5.0 %collective-permute-start.15 = (f32[64,256]{1,0:T(8,128)S(1)}, f32[64,256]{1,0:T(8,128)S(1)}, u32[]{:S(2)}, u32[]{:S(2)}) collective-permute-start(f32[64,256]{1,0:T(8,128)S(1)} %add.106), channel_id=1, source_target_pairs={{0,1},{1,0},{2,3},{3,2},{4,5},{5,4},{6,7},{7,6},{8,9},{9,8},{10,11... | collective-permute-start | bytes 196616 | tf_op jit(solution)/shard_map/ppermute | solution.py:179
  67.6 5.2 %collective-permute-start.27 = (f32[64,256]{1,0:T(8,128)S(1)}, f32[64,256]{1,0:T(8,128)S(1)}, u32[]{:S(2)}, u32[]{:S(2)}) collective-permute-start(f32[64,256]{1,0:T(8,128)S(1)} %add.121), channel_id=1, source_target_pairs={{0,3},{1,2},{2,1},{3,0},{4,7},{5,6},{6,5},{7,4},{8,11},{9,10},{10,... | collective-permute-start | bytes 196616 | tf_op jit(solution)/shard_map/ppermute | solution.py:179
  69.9 4.3 %collective-permute-start.26 = (f32[64,256]{1,0:T(8,128)S(1)}, f32[64,256]{1,0:T(8,128)S(1)}, u32[]{:S(2)}, u32[]{:S(2)}) collective-permute-start(f32[64,256]{1,0:T(8,128)S(1)} %add.121), channel_id=1, source_target_pairs={{0,2},{1,3},{2,0},{3,1},{4,6},{5,7},{6,4},{7,5},{8,10},{9,11},{10,... | collective-permute-start | bytes 196616 | tf_op jit(solution)/shard_map/ppermute | solution.py:179
  70.5 4.3 %collective-permute-start.25 = (f32[64,256]{1,0:T(8,128)S(1)}, f32[64,256]{1,0:T(8,128)S(1)}, u32[]{:S(2)}, u32[]{:S(2)}) collective-permute-start(f32[64,256]{1,0:T(8,128)S(1)} %add.121), channel_id=1, source_target_pairs={{0,1},{1,0},{2,3},{3,2},{4,5},{5,4},{6,7},{7,6},{8,9},{9,8},{10,11... | collective-permute-start | bytes 196616 | tf_op jit(solution)/shard_map/ppermute | solution.py:179
  71.2 4.7 %collective-permute-start.18 = (f32[256,256]{1,0:T(8,128)S(1)}, f32[256,256]{1,0:T(8,128)S(1)}, u32[]{:S(2)}, u32[]{:S(2)}) collective-permute-start(f32[256,256]{1,0:T(8,128)S(1)} %pad_maximum_fusion.own_ref), channel_id=1, source_target_pairs={{0,4},{4,0},{8,12},{12,8},{16,20},{20,16},{24,28},{28,24},{1,5},{5... | collective-permute-start | bytes 786440 | tf_op jit(solution)/shard_map/ppermute | solution.py:179
  74.8 5.5 %collective-permute-start.28 = (f32[256,256]{1,0:T(8,128)S(1)}, f32[256,256]{1,0:T(8,128)S(1)}, u32[]{:S(2)}, u32[]{:S(2)}) collective-permute-start(f32[256,256]{1,0:T(8,128)S(1)} %pad_maximum_fusion.1.own_ref), channel_id=1, source_target_pairs={{0,4},{4,0},{8,12},{12,8},{16,20},{20,16},{24,28},{28,24},{1,5},{5... | collective-permute-start | bytes 786440 | tf_op jit(solution)/shard_map/ppermute | solution.py:179
  74.9 15.3 %collective-permute-start.14 = (f32[512,128]{1,0:T(8,128)S(1)}, f32[512,128]{1,0:T(8,128)S(1)}, u32[]{:S(2)}, u32[]{:S(2)}) collective-permute-start(f32[512,128]{1,0:T(8,128)S(1)} %slice_add_fusion.2), channel_id=1, source_target_pairs={{0,16},{4,20},{8,24},{12,28},{16,0},{20,4},{24,8},{28,12},{1,17},{... | collective-permute-start | bytes 786440 | tf_op jit(solution)/shard_map/ppermute | solution.py:179
  80.3 9.9 %copy-start.5 = (s32[512]{0:T(512)S(1)}, s32[512]{0:T(512)}, u32[]{:S(2)}) copy-start(s32[512]{0:T(512)} %param.7) | copy-start | bytes 6148
  80.3 9.9 %copy-start.6 = (f32[128,1]{0,1:T(1,128)S(1)}, f32[128,1]{0,1:T(1,128)}, u32[]{:S(2)}) copy-start(f32[128,1]{0,1:T(1,128)} %param.6) | copy-start | bytes 1540
